TPU v7x, 32 devices: a whole 2x2x4 slice. The times are simulated.
32 devices in a mesh: row: 8 (over z, y), col: 4 (over x, core).
Axes of the slice: x: 2, y: 2, z: 4, core: 2. Of those that a mesh axis runs over, the one named last changes fastest.
Arguments:
- a_send: bfloat16 [2, 32, 32, 128, 128], P(None, ('row', 'col')), may hold values from -6 to 6
- a_where: int32 [2, 32, 32], P(None, ('row', 'col')), may hold values from -1 to 255, as said below
- b_strips: bfloat16 [8, 4, 16, 8, 128, 128], P('row', 'col'), may hold values from -0.25 to 0.25
- b_cols: int32 [8, 4, 16, 8], P('row', 'col'), may hold values from -1 to 7, as said below
Outputs:
- c_panel: bfloat16 [16384, 4096], P('row', 'col')
Inputs may be any that keep to these rules, and one draw needn't show every extreme that they name: `a_where`: positions named within one panel half of one grid device are distinct. Each panel half of each grid device has at least 12 and at most 24 named slots, and in every draw some have exactly 24. `b_cols`: block columns named within one block row of one panel are distinct. Each block row has at least 4 named slots, and in every draw some have exactly 8; the named slots lie anywhere in the row.
All inputs are finite; a program needn't handle non-finite values.
Results may differ from a plain program's by a relative error of at most 0.001.
Values may be sent and summed in bfloat16 or wider, within the bound.
No kernel may reach another device: no remote copies, remote signals or barrier semaphores. Data moves between devices by JAX's collectives and lax.ppermute only.
A program may use at most 128 MiB of HBM per device.

v0:
```python
import functools

import jax
import jax.numpy as jnp
from jax import lax
from jax.experimental import pallas as pl
from jax.experimental.pallas import tpu as pltpu
from jax.sharding import PartitionSpec as P

RB = 16
KB = 16
NJ = 8
PARTS = (64, 24, 8, 8, 24)
ALWAYS = PARTS[0] + PARTS[1]
LENT = 16
GROUP = 4
IN_SMEM = pl.BlockSpec(memory_space=pltpu.SMEM)
ANYWHERE = pl.BlockSpec(memory_space=pl.ANY)
LIMIT = 24 * 1024 * 1024


def in_hbm(value):
    return pltpu.with_memory_space_constraint(value, pltpu.HBM)


def places_in(table, half, owner):
    at = half * table.shape[0] + owner
    return lambda source: table[source, 1 + at // 128, at % 128]


def columns_in(table, rcap, device):
    return lambda slot: table[device, 0, slot % rcap * KB + slot // rcap]


def mark_rows(place, slots, named):
    def reset(j, carry):
        named[j] = 0
        return carry

    def mark(s, carry):
        here = place(s)

        @pl.when(here >= 0)
        def _():
            named[here % KB] = 1

        return carry

    lax.fori_loop(0, KB, reset, 0)
    lax.fori_loop(0, slots, mark, 0)


def for_wanted(column, named, rcap, action):
    def visit(slot, number):
        wanted = (column(slot) >= 0) & (named[slot // rcap] > 0)

        @pl.when(wanted)
        def _():
            action(slot, number)

        return number + wanted.astype(jnp.int32)

    return lax.fori_loop(0, KB * rcap, visit, 0)


def pack_main(spot, tables, strips, guests, *refs):
    early, late, stage, table, sem_table, named, sem, sem_out = refs[-8:]
    shift = spot[5]
    stop = stage.shape[0] - shift

    def greet(number, carry):
        pltpu.make_async_copy(guests.at[number], stage.at[number], sem).start()
        return carry

    lax.fori_loop(0, shift, greet, 0)

    def fetch(slot, number):
        @pl.when(number < stop)
        def _():
            pltpu.make_async_copy(strips.at[slot], stage.at[number + shift], sem).start()

    count = find_wanted(spot, tables, strips, table, sem_table, named, fetch)
    finish_blocks(strips, stage, sem, jnp.minimum(count, stop) + shift)
    hand_over(stage, [early, late], sem_out)


def pack_spare(spot, tables, strips, guests, *refs):
    *over, stage, table, sem_table, named, sem, sem_out = refs
    lent = spot[6]

    def fetch(slot, number):
        beyond = number - ALWAYS

        @pl.when((beyond >= 0) & (beyond < LENT))
        def _():
            pltpu.make_async_copy(strips.at[slot], stage.at[beyond], sem).start()

        @pl.when(beyond >= lent)
        def _():
            at = LENT + beyond - lent
            pltpu.make_async_copy(strips.at[slot], stage.at[at], sem).start()

    count = find_wanted(spot, tables, strips, table, sem_table, named, fetch)
    beyond = jnp.maximum(count - ALWAYS, 0)
    copied = jnp.minimum(beyond, LENT) + jnp.maximum(beyond - lent, 0)
    finish_blocks(strips, stage, sem, copied)
    hand_over(stage, [guests, *over], sem_out)


def find_wanted(spot, tables, strips, table, sem_table, named, action):
    rcap = strips.shape[0] // KB
    table_copy = pltpu.make_async_copy(tables, table, sem_table)
    table_copy.start()
    table_copy.wait()
    mark_rows(places_in(table, spot[0], spot[3]), table.shape[0], named)
    return for_wanted(columns_in(table, rcap, spot[1]), named, rcap, action)


def finish_blocks(source, target, sem, count):
    def finish(number, carry):
        pltpu.make_async_copy(source.at[0], target.at[0], sem).wait()
        return carry

    lax.fori_loop(0, count, finish, 0)


def hand_over(stage, outs, sem_out):
    copies, low = [], 0
    for i, out in enumerate(outs):
        here = stage.at[pl.ds(low, out.shape[0])]
        copies.append(pltpu.make_async_copy(here, out, sem_out.at[i]))
        copies[-1].start()
        low += out.shape[0]
    for copy in copies:
        copy.wait()


def pack(kernel, counts, spot, tables, strips, *more):
    size = strips.shape[-1]
    return pl.pallas_call(
        kernel,
        out_shape=[pltpu.HBM((n, size, size), strips.dtype) for n in counts],
        grid_spec=pltpu.PrefetchScalarGridSpec(
            num_scalar_prefetch=1,
            grid=(1,),
            in_specs=[ANYWHERE] * (2 + len(more)),
            out_specs=[ANYWHERE] * len(counts),
            scratch_shapes=[
                pltpu.VMEM((sum(counts), size, size), strips.dtype),
                pltpu.SMEM(tables.shape, jnp.int32),
                pltpu.SemaphoreType.DMA,
                pltpu.SMEM((KB,), jnp.int32),
                pltpu.SemaphoreType.DMA,
                pltpu.SemaphoreType.DMA((len(counts),)),
            ],
        ),
        compiler_params=pltpu.CompilerParams(vmem_limit_bytes=LIMIT),
        cost_estimate=pl.CostEstimate(
            flops=0, bytes_accessed=4 * sum(counts) * size * size, transcendentals=0
        ),
    )(spot, tables, in_hbm(strips), *more)


def after(value, blocks):
    count = len(blocks)
    return pl.pallas_call(
        lambda *refs: None,
        out_shape=[pltpu.HBM(each.shape, each.dtype) for each in blocks],
        in_specs=[ANYWHERE] * (count + 1),
        out_specs=[ANYWHERE] * count,
        input_output_aliases={i: i for i in range(count)},
    )(*blocks, value)


def by_block_row(place, slots, order, first):
    def reset(i, carry):
        first[i] = 0
        return carry

    def count(s, carry):
        here = place(s)

        @pl.when(here >= 0)
        def _():
            i = here // KB + 2
            first[i] = first[i] + 1

        return carry

    def scan(i, carry):
        first[i] = first[i] + first[i - 1]
        return carry

    def sort(s, carry):
        here = place(s)

        @pl.when(here >= 0)
        def _():
            i = here // KB + 1
            order[first[i]] = s * KB + here % KB
            first[i] = first[i] + 1

        return carry

    lax.fori_loop(0, RB + 2, reset, 0)
    lax.fori_loop(0, slots, count, 0)
    lax.fori_loop(1, RB + 2, scan, 0)
    lax.fori_loop(0, slots, sort, 0)


def clear(right, low):
    def one(j, carry):
        right[j] = jnp.zeros(right.shape[1:], right.dtype)
        return carry

    lax.fori_loop(low, KB, one, 0)


def add_rows(left, right, total, order, first):
    size = left.shape[1]

    def one_row(i, carry):
        row = pl.program_id(0) * GROUP + i
        here = pl.ds(pl.multiple_of(i * size, size), size)

        def add(entry, carry):
            total[here, :] += jnp.dot(
                left[order[entry] // KB], right[order[entry] % KB],
                preferred_element_type=jnp.float32,
            )
            return carry

        return lax.fori_loop(first[row], first[row + 1], add, carry)

    lax.fori_loop(0, GROUP, one_row, 0)


def place_at(right, where):
    size = right.shape[1]
    start = pl.multiple_of((where % NJ) * size, size)
    return right.at[where // NJ, :, pl.ds(start, size)]


def finish_right(source, right, sem, count):
    def finish(number, carry):
        pltpu.make_async_copy(source, place_at(right, 0), sem).wait()
        return carry

    lax.fori_loop(0, count, finish, 0)


def first_kernel(
    rcap, spot, tables, received, strips,
    out, next_order, next_first, next_target,
    left, right, table, sem_table, order, first, named, other, sem_left, sem_right,
):
    slots, size, _ = left.shape

    @pl.when(pl.program_id(0) == 0)
    def _():
        left_copy = pltpu.make_async_copy(received.at[:, pl.ds(0, size)], left, sem_left)
        left_copy.start()
        table_copy = pltpu.make_async_copy(tables, table, sem_table)
        table_copy.start()
        clear(right, 0)
        table_copy.wait()
        place = places_in(table, 0, spot[1])
        column = columns_in(table, rcap, spot[1])
        mark_rows(place, slots, named)

        def fetch(slot, number):
            target = place_at(right, slot // rcap * NJ + column(slot))
            pltpu.make_async_copy(strips.at[slot], target, sem_right).start()

        count = for_wanted(column, named, rcap, fetch)
        by_block_row(place, slots, order, first)

        next_place = places_in(table, spot[0], spot[2])
        next_column = columns_in(table, rcap, spot[4])
        by_block_row(next_place, slots, next_order, next_first)
        mark_rows(next_place, slots, other)

        def note(slot, number):
            next_target[number] = slot // rcap * NJ + next_column(slot)

        next_first[RB + 2] = for_wanted(next_column, other, rcap, note)
        left_copy.wait()
        finish_right(strips.at[0], right, sem_right, count)

    out[...] = jnp.zeros(out.shape, out.dtype)
    add_rows(left, right, out, order, first)


def start_left(shifted, parts, left, on_last, sem):
    size = left.shape[1]
    step = shifted.shape[1] - size
    whole = pltpu.make_async_copy(shifted.at[:, pl.ds(0, size)], left, sem)

    @pl.when(on_last)
    def _():
        for q, part in enumerate([shifted.at[:, pl.ds(size, step)], *parts]):
            pltpu.make_async_copy(part, left.at[:, pl.ds(q * step, step)], sem).start()

    @pl.when(jnp.logical_not(on_last))
    def _():
        whole.start()

    return whole


def start_right(sources, begin, count, target, right, sem):
    clear(right, jnp.where(count > begin, target[begin] // NJ, KB))
    for blocks, low, start, stop in sources:

        def fetch(number, carry):
            pltpu.make_async_copy(
                blocks.at[number - low], place_at(right, target[number]), sem
            ).start()
            return carry

        lax.fori_loop(start, jnp.minimum(count, stop), fetch, 0)


def add_products(row, order, first, left, right, touched, total):
    def add(entry, carry):
        @pl.when(touched[order[entry] % KB] > 0)
        def _():
            total[row] += jnp.dot(
                left[order[entry] // KB], right[order[entry] % KB],
                preferred_element_type=jnp.float32,
            )

        return carry

    lax.fori_loop(first[row], first[row + 1], add, 0)


def mark_targets(target, begin, end, marks):
    def reset(j, carry):
        marks[j] = 0
        return carry

    def mark(number, carry):
        marks[target[number] // NJ] = 1
        return carry

    lax.fori_loop(0, KB, reset, 0)
    lax.fori_loop(begin, end, mark, 0)


def mark_open(order, first, touched, open_row):
    def one(row, carry):
        def look(entry, found):
            return jnp.maximum(found, touched[order[entry] % KB])

        open_row[row] = lax.fori_loop(first[row], first[row + 1], look, jnp.int32(0))
        return carry

    lax.fori_loop(0, RB, one, 0)


def strip_of(ref, row, size):
    return ref.at[pl.ds(pl.multiple_of(row * size, size), size)]


def middle_kernel(parts_count, order, first, target, flags, *refs):
    shifted, *parts = refs[: 1 + parts_count]
    (
        piece, prev, out, rounded, guests, later, open_row,
        hall, sem_in, sem_home,
        left, right, total, short, touched,
        sem_left, sem_right, sem_prev, sem_out,
    ) = refs[1 + parts_count :]
    arrive = pltpu.make_async_copy(piece.at[pl.ds(0, LENT)], hall, sem_in)
    leave = pltpu.make_async_copy(hall, guests, sem_home)
    arrive.start()
    size = left.shape[1]
    count = first[RB + 2]
    shift = flags[1]
    end = piece.shape[0] - shift

    def prev_copy(row):
        return pltpu.make_async_copy(strip_of(prev, row, size), total.at[row], sem_prev.at[row])

    def start_prev(row, carry):
        prev_copy(row).start()
        return carry

    lax.fori_loop(0, RB, start_prev, 0)
    whole = start_left(shifted, parts, left, flags[0] > 0, sem_left)
    fetched = jnp.minimum(count, end)
    start_right([(piece, -shift, 0, end)], 0, fetched, target, right, sem_right)
    arrive.wait()
    leave.start()

    mark_targets(target, 0, fetched, touched)
    mark_targets(target, end, count, later)
    mark_open(order, first, later, open_row)
    whole.wait()
    finish_right(piece.at[0], right, sem_right, fetched)

    def out_copies(row):
        return (
            pltpu.make_async_copy(total.at[row], strip_of(out, row, size), sem_out.at[row]),
            pltpu.make_async_copy(short.at[row], strip_of(rounded, row, size), sem_out.at[row]),
        )

    def one_row(row, carry):
        open_copy, closed_copy = out_copies(row)
        prev_copy(row).wait()
        add_products(row, order, first, left, right, touched, total)

        @pl.when(open_row[row] > 0)
        def _():
            open_copy.start()

        @pl.when(open_row[row] == 0)
        def _():
            short[row] = total[row].astype(short.dtype)
            closed_copy.start()

        return carry

    def close_row(row, carry):
        open_copy, closed_copy = out_copies(row)

        @pl.when(open_row[row] > 0)
        def _():
            open_copy.wait()

        @pl.when(open_row[row] == 0)
        def _():
            closed_copy.wait()

        return carry

    lax.fori_loop(0, RB, one_row, 0)
    lax.fori_loop(0, RB, close_row, 0)
    leave.wait()


def last_kernel(parts_count, order, first, target, flags, touched, open_row, *refs):
    shifted, *parts = refs[: 1 + parts_count]
    (
        piece, back, *over, prev, _, out,
        left, right, total, short,
        sem_left, sem_right, sem_prev, sem_out,
    ) = refs[1 + parts_count :]
    size = left.shape[1]
    count = first[RB + 2]
    shift, lent = flags[1], flags[2]
    begin = PARTS[0] - shift

    def prev_copy(row):
        return pltpu.make_async_copy(strip_of(prev, row, size), total.at[row], sem_prev.at[row])

    def start_prev(row, carry):
        @pl.when(open_row[row] > 0)
        def _():
            prev_copy(row).start()

        return carry

    lax.fori_loop(0, RB, start_prev, 0)
    whole = start_left(shifted, parts, left, flags[0] > 0, sem_left)
    low = ALWAYS
    sources = [(piece, begin, begin, low - shift), (back, low, low, low + lent)]
    low = low + lent
    for blocks in over:
        high = low + blocks.shape[0]
        sources.append((blocks, low, low, high))
        low = high
    start_right(sources, begin, count, target, right, sem_right)

    def out_copy(row):
        return pltpu.make_async_copy(short.at[row], strip_of(out, row, size), sem_out.at[row])

    whole.wait()
    finish_right(piece.at[0], right, sem_right, count - begin)

    def one_row(row, carry):
        @pl.when(open_row[row] > 0)
        def _():
            prev_copy(row).wait()
            add_products(row, order, first, left, right, touched, total)
            short[row] = total[row].astype(short.dtype)
            out_copy(row).start()

        return carry

    def close_row(row, carry):
        @pl.when(open_row[row] > 0)
        def _():
            out_copy(row).wait()

        return carry

    lax.fori_loop(0, RB, one_row, 0)
    lax.fori_loop(0, RB, close_row, 0)


def step_call(kernel, scalars, operands, specs, out_shape, out_specs, scratch, slots, size):
    return pl.pallas_call(
        kernel,
        out_shape=out_shape,
        grid_spec=pltpu.PrefetchScalarGridSpec(
            num_scalar_prefetch=len(scalars),
            grid=(RB // GROUP,),
            in_specs=specs,
            out_specs=out_specs,
            scratch_shapes=[
                pltpu.VMEM((slots, size, size), jnp.bfloat16),
                pltpu.VMEM((KB, size, NJ * size), jnp.bfloat16),
                *scratch,
                pltpu.SemaphoreType.DMA,
                pltpu.SemaphoreType.DMA,
            ],
        ),
        compiler_params=pltpu.CompilerParams(
            dimension_semantics=("arbitrary",), vmem_limit_bytes=LIMIT
        ),
        cost_estimate=pl.CostEstimate(
            flops=2 * 24 * NJ * size * size * size,
            bytes_accessed=16 * 1024 * 1024,
            transcendentals=0,
        ),
    )(*scalars, *operands)


def table_kernel(where_ref, cols_ref, out, where, cols, tile, sems):
    copies = [
        pltpu.make_async_copy(where_ref, where, sems.at[0]),
        pltpu.make_async_copy(cols_ref, cols, sems.at[1]),
    ]
    for copy in copies:
        copy.start()
    rcap, across = cols.shape
    devices = where.shape[-1]
    tile[...] = jnp.zeros(tile.shape, tile.dtype)
    for copy in copies:
        copy.wait()
    for slot in range(rcap):
        tile[pl.ds(0, 1), pl.ds(slot * across, across)] = cols[pl.ds(slot, 1), :]
    for half in range(2):
        row, lane = divmod(half * devices, 128)
        tile[pl.ds(1 + row, 1), pl.ds(lane, devices)] = where[half]

    def fill(device, carry):
        out[device] = tile[...]
        return carry

    lax.fori_loop(0, out.shape[0], fill, 0)


def table_for_all(where, cols):
    devices = where.shape[-1]
    shape = (1 + -(-2 * devices // 128), 128)
    return pl.pallas_call(
        table_kernel,
        out_shape=jax.ShapeDtypeStruct((devices, *shape), jnp.int32),
        in_specs=[ANYWHERE, ANYWHERE],
        scratch_shapes=[
            pltpu.VMEM(where.shape, jnp.int32),
            pltpu.VMEM(cols.shape, jnp.int32),
            pltpu.VMEM(shape, jnp.int32),
            pltpu.SemaphoreType.DMA((2,)),
        ],
        compiler_params=pltpu.CompilerParams(vmem_limit_bytes=LIMIT),
    )(in_hbm(where), in_hbm(cols))


def needed(where_all, cols_all, rows_count, cols_count):
    grid = where_all.reshape(-1, 2, rows_count, cols_count)
    after = jnp.concatenate([grid[:, 0, :, 1:], grid[:, 1, :, :1]], axis=-1)
    columns = jnp.arange(KB, dtype=jnp.int32)
    hit = (after[..., None] >= 0) & (after[..., None] % KB == columns)
    wanted = jnp.any(hit, axis=0).astype(jnp.int32)
    counts = jnp.sum((cols_all >= 0).astype(jnp.int32), axis=1)
    counts = jnp.roll(counts.reshape(rows_count, cols_count, KB), -1, axis=0)
    return jnp.sum(wanted * counts, axis=-1)


def swapped(value):
    return lax.ppermute(value, "col", [(i, i ^ 1) for i in range(lax.axis_size("col"))])


def local(a_send, a_where, b_strips, b_cols):
    size = a_send.shape[-1]
    rows_count = lax.axis_size("row")
    cols_count = lax.axis_size("col")
    devices = rows_count * cols_count
    both = ("row", "col")
    row_index = lax.axis_index("row")
    col_index = lax.axis_index("col")
    rcap = b_strips.shape[3]
    last = cols_count - 1

    by_slot = jnp.swapaxes(b_cols, 2, 3).reshape(rcap, KB)
    tables = lax.all_to_all(
        table_for_all(a_where, by_slot), both, split_axis=0, concat_axis=0, tiled=True
    )
    after_col = (col_index + 1) % cols_count
    after_half = (col_index + 1) // cols_count
    row_before = (row_index + rows_count - 1) % rows_count
    row_after = (row_index + 1) % rows_count
    needs = needed(
        tables[:, 1:].reshape(devices, -1)[:, : 2 * devices],
        tables[:, 0].reshape(devices, rcap, KB), rows_count, cols_count,
    )
    room = ALWAYS - jnp.flip(needs.reshape(rows_count, -1, 2), -1).reshape(needs.shape)
    lent = jnp.maximum(jnp.minimum(jnp.minimum(needs - ALWAYS, room), LENT), 0)
    most = jnp.max(needs - lent)

    def lent_to(row, col):
        return lax.dynamic_slice(lent, (row, col), (1, 1))[0, 0]

    spot = jnp.stack([
        after_half,
        row_index * cols_count + col_index,
        row_index * cols_count + after_col,
        row_before * cols_count + after_col,
        row_after * cols_count + col_index,
        lent_to(row_before, col_index ^ 1),
        lent_to(row_before, col_index),
    ]).astype(jnp.int32)

    wrapped = a_send[1, 0].reshape(rows_count, cols_count, size, size)[:, 0]
    wrapped = wrapped.reshape(devices, size // cols_count, size)
    received = lax.all_to_all(
        jnp.concatenate([a_send[0, 0], wrapped], axis=1),
        both, split_axis=0, concat_axis=0, tiled=True,
    )

    def to_row_before(blocks):
        return lax.ppermute(
            blocks, "row", [(i, (i - 1) % rows_count) for i in range(rows_count)]
        )

    strips = b_strips.reshape(KB * rcap, size, size)
    guests, *over = pack(pack_spare, (LENT, *PARTS[2:]), spot, tables, strips)
    begin, extra = ALWAYS, []
    for blocks in over:
        extra.append(lax.cond(most > begin, to_row_before, lambda same: same, blocks))
        begin += blocks.shape[0]
    early, late = pack(
        pack_main, PARTS[:2], spot, tables, strips, swapped(guests),
        *(blocks[0, :16] for blocks in extra),
    )
    early, late = map(to_row_before, after(received[0, :16], [early, late]))

    shifted = lax.ppermute(
        received, "col", [(i, (i - 1) % cols_count) for i in range(cols_count)]
    )
    part = received[:, size:]
    parts = [lax.ppermute(part, "col", [(i, last)]) for i in range(1, last)] + [part]

    wide = NJ * size
    strip = pl.BlockSpec((GROUP * size, wide), lambda i, *_: (i, 0))
    begun, order, first, target = step_call(
        functools.partial(first_kernel, rcap),
        (spot,), (tables, received, in_hbm(strips)), [ANYWHERE, ANYWHERE, ANYWHERE],
        [
            pltpu.HBM((RB * size, wide), jnp.float32),
            jax.ShapeDtypeStruct((devices,), jnp.int32),
            jax.ShapeDtypeStruct((RB + 3,), jnp.int32),
            jax.ShapeDtypeStruct((KB * rcap,), jnp.int32),
        ],
        [strip, IN_SMEM, IN_SMEM, IN_SMEM],
        [
            pltpu.SMEM(tables.shape, jnp.int32),
            pltpu.SemaphoreType.DMA,
            pltpu.SMEM((devices,), jnp.int32),
            pltpu.SMEM((RB + 2,), jnp.int32),
            pltpu.SMEM((KB,), jnp.int32),
            pltpu.SMEM((KB,), jnp.int32),
        ],
        devices, size,
    )

    on_last = (col_index == last).astype(jnp.int32)
    lent_here = [lent_to(row_index, col_index ^ 1), lent_to(row_index, col_index)]
    scalars = (order, first, target, jnp.stack([on_last, *lent_here]))
    lefts = (shifted, *parts)

    def finish_call(kernel, scalars, operands, out_shape, out_specs, scratch, marks, aliases):
        return pl.pallas_call(
            kernel,
            out_shape=out_shape,
            grid_spec=pltpu.PrefetchScalarGridSpec(
                num_scalar_prefetch=len(scalars),
                grid=(1,),
                in_specs=[ANYWHERE] * len(operands),
                out_specs=out_specs,
                scratch_shapes=[
                    *scratch,
                    pltpu.VMEM((devices, size, size), jnp.bfloat16),
                    pltpu.VMEM((KB, size, wide), jnp.bfloat16),
                    pltpu.VMEM((RB, size, wide), jnp.float32),
                    pltpu.VMEM((RB, size, wide), jnp.bfloat16),
                    *marks,
                    pltpu.SemaphoreType.DMA,
                    pltpu.SemaphoreType.DMA,
                    pltpu.SemaphoreType.DMA((RB,)),
                    pltpu.SemaphoreType.DMA((RB,)),
                ],
            ),
            input_output_aliases=aliases,
            compiler_params=pltpu.CompilerParams(vmem_limit_bytes=LIMIT),
            cost_estimate=pl.CostEstimate(
                flops=2 * 16 * NJ * size * size * size,
                bytes_accessed=12 * 1024 * 1024,
                transcendentals=0,
            ),
        )(*scalars, *operands)

    begun, rounded, guests, later, open_row = finish_call(
        functools.partial(middle_kernel, len(parts)), scalars,
        (*lefts, early, in_hbm(begun)),
        [
            pltpu.HBM((RB * size, wide), jnp.float32),
            pltpu.HBM((RB * size, wide), jnp.bfloat16),
            pltpu.HBM((LENT, size, size), jnp.bfloat16),
            jax.ShapeDtypeStruct((KB,), jnp.int32),
            jax.ShapeDtypeStruct((RB,), jnp.int32),
        ],
        [ANYWHERE, ANYWHERE, ANYWHERE, IN_SMEM, IN_SMEM],
        [
            pltpu.VMEM((LENT, size, size), jnp.bfloat16),
            pltpu.SemaphoreType.DMA,
            pltpu.SemaphoreType.DMA,
        ],
        [pltpu.SMEM((KB,), jnp.int32)], {},
    )
    back = swapped(guests)

    operands = (*lefts, late, back, *extra, in_hbm(begun), rounded)
    scalars = (*scalars, later, open_row)
    return finish_call(
        functools.partial(last_kernel, len(parts)), scalars, operands,
        jax.ShapeDtypeStruct((RB * size, wide), jnp.bfloat16),
        ANYWHERE, [], [], {len(scalars) + len(operands) - 1: 0},
    )


def solution(mesh):
    placed = (
        P(None, ("row", "col"), None, None, None),
        P(None, ("row", "col"), None),
        P("row", "col", None, None, None, None),
        P("row", "col", None, None),
    )
    return jax.shard_map(
        local, mesh=mesh, in_specs=placed, out_specs=P("row", "col"), check_vma=False
    )
```

profile of v0, /device:TPU:30, one launch (start us, length us, event | category | flops | bytes accessed | tf_op | source)
XLA Modules:
  0.0 121.3 jit_solution(17122356737250294863)
XLA Ops:
  0.0 1.6 %shard_map.46 = s32[32,2,128]{2,1,0:T(2,128)} custom-call(s32[2,1,32]{2,1,0:T(1,128)} %where_ref.1, s32[8,16]{1,0:T(8,128)} %bitcast.58), custom_call_target="tpu_custom_call" | custom-call | tf_op jit(solution)/shard_map/pallas_call | solution.py:558
  1.6 5.8 %all-to-all-start = ((s32[32,2,128]{2,1,0:T(2,128)}), s32[32,2,128]{2,1,0:T(2,128)S(1)}, u32[]{:S(2)}, u32[]{:S(2)}) async-start(s32[32,2,128]{2,1,0:T(2,128)} %shard_map.46), calls=%async_computation | async-start | bytes 65536 | tf_op jit(solution)/shard_map/all_to_all | solution.py:599
  7.4 1.7 %slice_bitcast_fusion = (bf16[32,128,128]{2,1,0:T(8,128)(2,1)S(1)}, bf16[1,1,32,128,128]{4,3,2,1,0:T(8,128)(2,1)S(1)}) fusion(bf16[2,1,32,128,128]{4,3,2,1,0:T(8,128)(2,1)} %param.10), kind=kLoop, calls=%fused_computation.1 | loop fusion | bytes 4194304 | tf_op jit(solution)/shard_map/squeeze | solution.py:630
  9.2 1.2 pad_maximum_fusion
  10.4 0.0 all-to-all-done.tables
  10.4 7.0 %all-to-all-start.1 = ((bf16[32,160,128]{2,1,0:T(8,128)(2,1)}), bf16[32,160,128]{2,1,0:T(8,128)(2,1)S(1)}, u32[]{:S(2)}, u32[]{:S(2)}) async-start(bf16[32,160,128]{2,1,0:T(8,128)(2,1)} %pad_maximum_fusion), calls=%async_computation.1 | async-start | bytes 2621440 | tf_op jit(solution)/shard_map/all_to_all | solution.py:629
  17.4 0.1 copy.34
  17.5 0.1 copy.37
  17.7 0.1 slice.93
  17.7 0.1 copy.39
  17.8 0.1 copy.38
  18.0 0.6 fusion.1
  18.6 0.2 fusion.3
  18.9 0.1 copy.40
  19.0 0.7 subtract_reduce_fusion
  19.7 0.1 copy.41
  19.8 0.7 fusion.5
  20.4 1.4 %stack.32.spot = s32[7]{0:T(128)S(1)} concatenate(s32[1]{0:T(128)} %bitcast, s32[1]{0:T(128)} %bitcast.1, s32[1]{0:T(128)} %bitcast.2, s32[1]{0:T(128)} %bitcast.3, s32[1]{0:T(128)} %bitcast.4, s32[1]{0:T(128)} %bitcast.17, s32[1]{0:T(128)} %bitcast.18), dimensions={0} | concatenate | bytes 56 | tf_op jit(solution)/shard_map/stack | solution.py:617
  21.8 5.8 %shard_map.48 = (bf16[16,128,128]{2,1,0:T(8,128)(2,1)}, bf16[8,128,128]{2,1,0:T(8,128)(2,1)}, bf16[8,128,128]{2,1,0:T(8,128)(2,1)}, bf16[24,128,128]{2,1,0:T(8,128)(2,1)}) custom-call(s32[7]{0:T(128)S(1)} %stack.32.spot, s32[32,2,128]{2,1,0:T(2,128)S(1)} %all-to-all-done.tables, bf16[128,128,128]{2,1,0:T(8,128)(2,1)} %bitcast.43), custom_call_target="tpu_custom_call" | custom-call | bytes 3670016 | tf_op jit(solution)/shard_map/pallas_call | solution.py:140
  27.7 0.2 collective-permute-start.6
  29.8 0.7 slice_bitcast_fusion.5.refs_0_
  30.5 0.7 slice_bitcast_fusion.3
  31.2 0.0 collective-permute-done.6.guests
  31.2 6.8 %shard_map.49 = (bf16[64,128,128]{2,1,0:T(8,128)(2,1)}, bf16[24,128,128]{2,1,0:T(8,128)(2,1)}) custom-call(s32[7]{0:T(128)S(1)} %stack.32.spot, s32[32,2,128]{2,1,0:T(2,128)S(1)} %all-to-all-done.tables, bf16[128,128,128]{2,1,0:T(8,128)(2,1)} %bitcast.44, bf16[16,128,128]{2,1,0:T(8,128)(2,1)S(1)} %collective-permute-done.6.guests, ...), custom_call_target="tpu_custom_call" | custom-call | bytes 5767168 | tf_op jit(solution)/shard_map/pallas_call | solution.py:140
  38.0 9.1 %all-to-all-done.1.received = bf16[32,160,128]{2,1,0:T(8,128)(2,1)S(1)} async-done(((bf16[32,160,128]{2,1,0:T(8,128)(2,1)}), bf16[32,160,128]{2,1,0:T(8,128)(2,1)S(1)}, u32[]{:S(2)}, u32[]{:S(2)}) %all-to-all-start.1) | async-done | bytes 1310752 | tf_op jit(solution)/shard_map/all_to_all | solution.py:629
  47.1 0.6 slice_bitcast_fusion.2.refs_2_
  47.7 0.4 collective-permute-start.7
  48.1 0.0 collective-permute-start.3
  48.1 2.4 %collective-permute-start.5 = (bf16[32,32,128]{2,1,0:T(8,128)(2,1)S(1)}, bf16[32,32,128]{2,1,0:T(8,128)(2,1)S(1)}, u32[]{:S(2)}, u32[]{:S(2)}) collective-permute-start(bf16[32,32,128]{2,1,0:T(8,128)(2,1)S(1)} %slice.96.refs_3_), channel_id=1, source_target_pairs={{2,3},{6,7},{10,11},{14,15},{18,19},{22,23},{26,27},{30,31}} | collective-permute-start | bytes 786440 | tf_op jit(solution)/shard_map/ppermute | solution.py:655
  50.5 0.7 collective-permute-start.4
  51.2 0.7 collective-permute-start.8
  51.9 1.4 %pad_add_fusion.1.flags = s32[3]{0:T(128)S(1)} fusion(s32[1]{0:T(128)} %bitcast.25, s32[1]{0:T(128)} %bitcast.24, s32[1]{0:T(128)} %bitcast.23), kind=kLoop, calls=%fused_computation.23 | loop fusion | flops 6 | bytes 24 | tf_op jit(solution)/shard_map/stack | solution.py:682
  53.3 20.6 %shard_map.47 = (f32[2048,1024]{1,0:T(8,128)}, s32[32]{0:T(128)S(1)}, s32[19]{0:T(128)S(1)}, s32[128]{0:T(128)S(1)}) custom-call(s32[7]{0:T(128)S(1)} %stack.32.spot, s32[32,2,128]{2,1,0:T(2,128)S(1)} %all-to-all-done.tables, bf16[32,160,128]{2,1,0:T(8,128)(2,1)S(1)} %all-to-all-done.1.received, bf16[128,128,128]{2,1,0:T(8,128)(2,1)} %bitcast.45), custom_call_target="tpu_custom_call" | custom-call | flops 805306368 | bytes 16777216 | tf_op jit(solution)/shard_map/pallas_call | solution.py:503
  73.9 0.0 collective-permute-done.5.refs_2_
  73.9 0.0 collective-permute-done.4.refs_1_
  73.9 0.0 collective-permute-done.3.refs_0_
  73.9 25.3 %collective-permute-done.7.refs_4_ = bf16[64,128,128]{2,1,0:T(8,128)(2,1)} collective-permute-done((bf16[64,128,128]{2,1,0:T(8,128)(2,1)}, bf16[64,128,128]{2,1,0:T(8,128)(2,1)}, u32[]{:S(2)}, u32[]{:S(2)}) %collective-permute-start.7) | collective-permute-done | bytes 2097184 | tf_op jit(solution)/shard_map/ppermute | solution.py:635
  99.2 0.0 copy-start
  99.2 0.0 copy-start.1
  99.2 0.0 copy-start.2
  99.2 10.0 %shard_map.51 = (f32[2048,1024]{1,0:T(8,128)}, bf16[2048,1024]{1,0:T(8,128)(2,1)}, bf16[16,128,128]{2,1,0:T(8,128)(2,1)}, s32[16]{0:T(128)S(1)}, s32[16]{0:T(128)S(1)}) custom-call(s32[32]{0:T(128)S(1)} %get-tuple-element.55.order, s32[19]{0:T(128)S(1)} %get-tuple-element.56.first, s32[128]{0:T(128)S(1)} %get-tuple-element.57.target, ...), custom_call_target="tpu_custom_call" | custom-call | flops 536870912 | bytes 12582912 | tf_op jit(solution)/shard_map/pallas_call | solution.py:686
  109.2 0.1 collective-permute-start.9
  109.3 5.9 %collective-permute-done.8.refs_4_ = bf16[24,128,128]{2,1,0:T(8,128)(2,1)} collective-permute-done((bf16[24,128,128]{2,1,0:T(8,128)(2,1)}, bf16[24,128,128]{2,1,0:T(8,128)(2,1)}, u32[]{:S(2)}, u32[]{:S(2)}) %collective-permute-start.8) | collective-permute-done | bytes 786464 | tf_op jit(solution)/shard_map/ppermute | solution.py:635
  115.2 0.0 collective-permute-done.9.refs_5_
  115.2 0.0 copy-done
  115.2 0.0 copy-done.1
  115.2 0.0 copy-done.2
  115.2 6.1 %shard_map.52 = bf16[2048,1024]{1,0:T(8,128)(2,1)} custom-call(s32[32]{0:T(128)S(1)} %get-tuple-element.55.order, s32[19]{0:T(128)S(1)} %get-tuple-element.56.first, s32[128]{0:T(128)S(1)} %get-tuple-element.57.target, s32[3]{0:T(128)S(1)} %pad_add_fusion.1.flags, s32[16]{0:T(128)S(1)} %get-tuple-element.66.touched, ...), custom_call_target="tpu_custom_call", output_to_operand_aliasing={{}: (16, {})} | custom-call | flops 536870912 | bytes 12582912 | tf_op jit(solution)/shard_map/pallas_call | solution.py:686
  (17 shorter events, 0.2 us)
Async XLA Ops:
  1.6 8.8 %all-to-all-start = ((s32[32,2,128]{2,1,0:T(2,128)}), s32[32,2,128]{2,1,0:T(2,128)S(1)}, u32[]{:S(2)}, u32[]{:S(2)}) async-start(s32[32,2,128]{2,1,0:T(2,128)} %shard_map.46), calls=%async_computation | async-start | bytes 65536 | tf_op jit(solution)/shard_map/all_to_all | solution.py:599
  10.4 36.7 %all-to-all-start.1 = ((bf16[32,160,128]{2,1,0:T(8,128)(2,1)}), bf16[32,160,128]{2,1,0:T(8,128)(2,1)S(1)}, u32[]{:S(2)}, u32[]{:S(2)}) async-start(bf16[32,160,128]{2,1,0:T(8,128)(2,1)} %pad_maximum_fusion), calls=%async_computation.1 | async-start | bytes 2621440 | tf_op jit(solution)/shard_map/all_to_all | solution.py:629
  27.7 3.5 %collective-permute-start.6 = (bf16[16,128,128]{2,1,0:T(8,128)(2,1)}, bf16[16,128,128]{2,1,0:T(8,128)(2,1)S(1)}, u32[]{:S(2)}, u32[]{:S(2)}) collective-permute-start(bf16[16,128,128]{2,1,0:T(8,128)(2,1)} %get-tuple-element.58), channel_id=1, source_target_pairs={{0,1},{1,0},{2,3},{3,2},{4,5},{5,4},{6,7},{7,6},{8,9},{9,8},{10,11... | collective-permute-start | bytes 1572872 | tf_op jit(solution)/shard_map/ppermute | solution.py:584
  47.7 51.5 %collective-permute-start.7 = (bf16[64,128,128]{2,1,0:T(8,128)(2,1)}, bf16[64,128,128]{2,1,0:T(8,128)(2,1)}, u32[]{:S(2)}, u32[]{:S(2)}) collective-permute-start(bf16[64,128,128]{2,1,0:T(8,128)(2,1)} %get-tuple-element.64), channel_id=1, source_target_pairs={{0,28},{4,0},{8,4},{12,8},{16,12},{20,16},{24,20},{28,24},{1,29},{... | collective-permute-start | bytes 6291464 | tf_op jit(solution)/shard_map/ppermute | solution.py:635
  48.1 25.8 %collective-permute-start.3 = (bf16[32,160,128]{2,1,0:T(8,128)(2,1)S(1)}, bf16[32,160,128]{2,1,0:T(8,128)(2,1)S(1)}, u32[]{:S(2)}, u32[]{:S(2)}) collective-permute-start(bf16[32,160,128]{2,1,0:T(8,128)(2,1)S(1)} %all-to-all-done.1.received), channel_id=1, source_target_pairs={{0,3},{1,0},{2,1},{3,2},{4,7},{5,4},{6,5},{7,6},{8,11},{9,8},{10,9... | collective-permute-start | bytes 3932168 | tf_op jit(solution)/shard_map/ppermute | solution.py:651
  48.1 25.8 %collective-permute-start.5 = (bf16[32,32,128]{2,1,0:T(8,128)(2,1)S(1)}, bf16[32,32,128]{2,1,0:T(8,128)(2,1)S(1)}, u32[]{:S(2)}, u32[]{:S(2)}) collective-permute-start(bf16[32,32,128]{2,1,0:T(8,128)(2,1)S(1)} %slice.96.refs_3_), channel_id=1, source_target_pairs={{2,3},{6,7},{10,11},{14,15},{18,19},{22,23},{26,27},{30,31}} | collective-permute-start | bytes 786440 | tf_op jit(solution)/shard_map/ppermute | solution.py:655
  50.5 23.4 %collective-permute-start.4 = (bf16[32,32,128]{2,1,0:T(8,128)(2,1)S(1)}, bf16[32,32,128]{2,1,0:T(8,128)(2,1)S(1)}, u32[]{:S(2)}, u32[]{:S(2)}) collective-permute-start(bf16[32,32,128]{2,1,0:T(8,128)(2,1)S(1)} %slice.96.refs_3_), channel_id=1, source_target_pairs={{1,3},{5,7},{9,11},{13,15},{17,19},{21,23},{25,27},{29,31}} | collective-permute-start | bytes 786440 | tf_op jit(solution)/shard_map/ppermute | solution.py:655
  51.2 63.9 %collective-permute-start.8 = (bf16[24,128,128]{2,1,0:T(8,128)(2,1)}, bf16[24,128,128]{2,1,0:T(8,128)(2,1)}, u32[]{:S(2)}, u32[]{:S(2)}) collective-permute-start(bf16[24,128,128]{2,1,0:T(8,128)(2,1)} %get-tuple-element.68), channel_id=1, source_target_pairs={{0,28},{4,0},{8,4},{12,8},{16,12},{20,16},{24,20},{28,24},{1,29},{... | collective-permute-start | bytes 2359304 | tf_op jit(solution)/shard_map/ppermute | solution.py:635
  99.2 16.0 %copy-start = (bf16[24,128,128]{2,1,0:T(8,128)(2,1)S(1)}, bf16[24,128,128]{2,1,0:T(8,128)(2,1)}, u32[]{:S(2)}) copy-start(bf16[24,128,128]{2,1,0:T(8,128)(2,1)} %get-tuple-element.84.refs_8_) | copy-start | bytes 2359300
  99.2 16.0 %copy-start.1 = (bf16[8,128,128]{2,1,0:T(8,128)(2,1)S(1)}, bf16[8,128,128]{2,1,0:T(8,128)(2,1)}, u32[]{:S(2)}) copy-start(bf16[8,128,128]{2,1,0:T(8,128)(2,1)} %get-tuple-element.83.refs_7_) | copy-start | bytes 786436
  99.2 16.0 %copy-start.2 = (bf16[8,128,128]{2,1,0:T(8,128)(2,1)S(1)}, bf16[8,128,128]{2,1,0:T(8,128)(2,1)}, u32[]{:S(2)}) copy-start(bf16[8,128,128]{2,1,0:T(8,128)(2,1)} %get-tuple-element.82.refs_6_) | copy-start | bytes 786436
  109.2 6.0 %collective-permute-start.9 = (bf16[16,128,128]{2,1,0:T(8,128)(2,1)}, bf16[16,128,128]{2,1,0:T(8,128)(2,1)S(1)}, u32[]{:S(2)}, u32[]{:S(2)}) collective-permute-start(bf16[16,128,128]{2,1,0:T(8,128)(2,1)} %get-tuple-element.69), channel_id=1, source_target_pairs={{0,1},{1,0},{2,3},{3,2},{4,5},{5,4},{6,7},{7,6},{8,9},{9,8},{10,11... | collective-permute-start | bytes 1572872 | tf_op jit(solution)/shard_map/ppermute | solution.py:584
where the time goes:
time: 121 us
  Pallas kernels  50.9 us (42%)
  waiting for transfers between devices  40.3 us (33%)
  starting transfers between devices  17.3 us (14%)
  local copies, waits for them, and re-layouts  6.45 us (5%)
  other arithmetic  4.2 us (3%)
  between operations  2.16 us (2%)
    ppermute x2, waiting for transfers between devices, to_row_before(): lax.ppermute(blocks, 'row', [(i, (i - 1) % rows_count) for i in range(row...  31.1 us
    pallas_call x1, Pallas kernels, step_call(): pl.pallas_call(kernel, out_shape=out_shape, grid_spec=pltpu.PrefetchScala...  20.6 us
    pallas_call x2, Pallas kernels, finish_call(): pl.pallas_call(kernel, out_shape=out_shape, grid_spec=pltpu.PrefetchScala...  16.1 us
    pallas_call x2, Pallas kernels, pack(): pl.pallas_call(kernel, out_shape=[pltpu.HBM((n, size, size), strips.dtype...  12.6 us
    all_to_all x1, waiting for transfers between devices, local(): lax.all_to_all(jnp.concatenate([a_send[0, 0], wrapped], axis=1), both, sp...  9.11 us
    all_to_all x1, starting transfers between devices, local(): lax.all_to_all(jnp.concatenate([a_send[0, 0], wrapped], axis=1), both, sp...  6.98 us
    all_to_all x1, starting transfers between devices, local(): lax.all_to_all(table_for_all(a_where, by_slot), both, split_axis=0, conca...  5.84 us
    ppermute x2, starting transfers between devices, local(): lax.ppermute(part, 'col', [(i, last)])  3.1 us
  transfers between devices with their start and end apart: 9, of which 3 were waited for; matrix products, arithmetic and copies ran while one was open for 8% of the time, Pallas kernels for 36%

commit v1 on v0

--- a/solution.py
+++ b/solution.py
@@ -10,8 +10,10 @@
 RB = 16
 KB = 16
 NJ = 8
-PARTS = (64, 24, 8, 8, 24)
-ALWAYS = PARTS[0] + PARTS[1]
+AHEAD = 16
+PARTS = (48, 24)
+OVER = (8, 8, 24)
+ALWAYS = AHEAD + sum(PARTS)
 LENT = 16
 GROUP = 4
 IN_SMEM = pl.BlockSpec(memory_space=pltpu.SMEM)
@@ -66,7 +68,7 @@
 def pack_main(spot, tables, strips, guests, *refs):
     early, late, stage, table, sem_table, named, sem, sem_out = refs[-8:]
     shift = spot[5]
-    stop = stage.shape[0] - shift
+    stop = ALWAYS - shift
 
     def greet(number, carry):
         pltpu.make_async_copy(guests.at[number], stage.at[number], sem).start()
@@ -75,36 +77,42 @@
     lax.fori_loop(0, shift, greet, 0)
 
     def fetch(slot, number):
-        @pl.when(number < stop)
-        def _():
-            pltpu.make_async_copy(strips.at[slot], stage.at[number + shift], sem).start()
+        @pl.when((number >= AHEAD) & (number < stop))
+        def _():
+            at = number - AHEAD + shift
+            pltpu.make_async_copy(strips.at[slot], stage.at[at], sem).start()
 
     count = find_wanted(spot, tables, strips, table, sem_table, named, fetch)
-    finish_blocks(strips, stage, sem, jnp.minimum(count, stop) + shift)
+    finish_blocks(strips, stage, sem, jnp.maximum(jnp.minimum(count, stop) - AHEAD, 0) + shift)
     hand_over(stage, [early, late], sem_out)
 
 
-def pack_spare(spot, tables, strips, guests, *refs):
+def pack_ahead(spot, tables, strips, ahead, guests, *refs):
     *over, stage, table, sem_table, named, sem, sem_out = refs
     lent = spot[6]
 
     def fetch(slot, number):
         beyond = number - ALWAYS
 
+        @pl.when(number < AHEAD)
+        def _():
+            pltpu.make_async_copy(strips.at[slot], stage.at[number], sem).start()
+
         @pl.when((beyond >= 0) & (beyond < LENT))
         def _():
-            pltpu.make_async_copy(strips.at[slot], stage.at[beyond], sem).start()
+            at = AHEAD + beyond
+            pltpu.make_async_copy(strips.at[slot], stage.at[at], sem).start()
 
         @pl.when(beyond >= lent)
         def _():
-            at = LENT + beyond - lent
+            at = AHEAD + LENT + beyond - lent
             pltpu.make_async_copy(strips.at[slot], stage.at[at], sem).start()
 
     count = find_wanted(spot, tables, strips, table, sem_table, named, fetch)
     beyond = jnp.maximum(count - ALWAYS, 0)
-    copied = jnp.minimum(beyond, LENT) + jnp.maximum(beyond - lent, 0)
-    finish_blocks(strips, stage, sem, copied)
-    hand_over(stage, [guests, *over], sem_out)
+    copied = jnp.minimum(count, AHEAD) + jnp.minimum(beyond, LENT)
+    finish_blocks(strips, stage, sem, copied + jnp.maximum(beyond - lent, 0))
+    hand_over(stage, [ahead, guests, *over], sem_out)
 
 
 def find_wanted(spot, tables, strips, table, sem_table, named, action):
@@ -366,7 +374,7 @@
 def middle_kernel(parts_count, order, first, target, flags, *refs):
     shifted, *parts = refs[: 1 + parts_count]
     (
-        piece, prev, out, rounded, guests, later, open_row,
+        ahead, piece, prev, out, rounded, guests, later, open_row,
         hall, sem_in, sem_home,
         left, right, total, short, touched,
         sem_left, sem_right, sem_prev, sem_out,
@@ -377,7 +385,7 @@
     size = left.shape[1]
     count = first[RB + 2]
     shift = flags[1]
-    end = piece.shape[0] - shift
+    end = AHEAD + PARTS[0] - shift
 
     def prev_copy(row):
         return pltpu.make_async_copy(strip_of(prev, row, size), total.at[row], sem_prev.at[row])
@@ -389,7 +397,8 @@
     lax.fori_loop(0, RB, start_prev, 0)
     whole = start_left(shifted, parts, left, flags[0] > 0, sem_left)
     fetched = jnp.minimum(count, end)
-    start_right([(piece, -shift, 0, end)], 0, fetched, target, right, sem_right)
+    sources = [(ahead, 0, 0, AHEAD), (piece, AHEAD - shift, AHEAD, end)]
+    start_right(sources, 0, fetched, target, right, sem_right)
     arrive.wait()
     leave.start()
 
@@ -449,7 +458,7 @@
     size = left.shape[1]
     count = first[RB + 2]
     shift, lent = flags[1], flags[2]
-    begin = PARTS[0] - shift
+    begin = AHEAD + PARTS[0] - shift
 
     def prev_copy(row):
         return pltpu.make_async_copy(strip_of(prev, row, size), total.at[row], sem_prev.at[row])
@@ -637,13 +646,14 @@
         )
 
     strips = b_strips.reshape(KB * rcap, size, size)
-    guests, *over = pack(pack_spare, (LENT, *PARTS[2:]), spot, tables, strips)
+    ahead, guests, *over = pack(pack_ahead, (AHEAD, LENT, *OVER), spot, tables, strips)
+    ahead = to_row_before(ahead)
     begin, extra = ALWAYS, []
     for blocks in over:
         extra.append(lax.cond(most > begin, to_row_before, lambda same: same, blocks))
         begin += blocks.shape[0]
     early, late = pack(
-        pack_main, PARTS[:2], spot, tables, strips, swapped(guests),
+        pack_main, PARTS, spot, tables, strips, swapped(guests),
         *(blocks[0, :16] for blocks in extra),
     )
     early, late = map(to_row_before, after(received[0, :16], [early, late]))
@@ -715,7 +725,7 @@
 
     begun, rounded, guests, later, open_row = finish_call(
         functools.partial(middle_kernel, len(parts)), scalars,
-        (*lefts, early, in_hbm(begun)),
+        (*lefts, ahead, early, in_hbm(begun)),
         [
             pltpu.HBM((RB * size, wide), jnp.float32),
             pltpu.HBM((RB * size, wide), jnp.bfloat16),

time: 121 us -> 144 us (1.19)
  the two profiles are of different devices: /device:TPU:30 before, /device:TPU:3 now
where the time goes in v1:
time: 144 us
  waiting for transfers between devices  55.6 us (39%)
  Pallas kernels  50.9 us (35%)
  starting transfers between devices  24.2 us (17%)
  local copies, waits for them, and re-layouts  7.26 us (5%)
  other arithmetic  4.07 us (3%)
  between operations  2.14 us (1%)
    ppermute x3, waiting for transfers between devices, to_row_before(): lax.ppermute(blocks, 'row', [(i, (i - 1) % rows_count) for i in range(row...  41.4 us
    pallas_call x1, Pallas kernels, step_call(): pl.pallas_call(kernel, out_shape=out_shape, grid_spec=pltpu.PrefetchScala...  19.4 us
    pallas_call x2, Pallas kernels, finish_call(): pl.pallas_call(kernel, out_shape=out_shape, grid_spec=pltpu.PrefetchScala...  16.5 us
    pallas_call x2, Pallas kernels, pack(): pl.pallas_call(kernel, out_shape=[pltpu.HBM((n, size, size), strips.dtype...  13.4 us
    all_to_all x1, waiting for transfers between devices, local(): lax.all_to_all(jnp.concatenate([a_send[0, 0], wrapped], axis=1), both, sp...  9.43 us
    ppermute x3, starting transfers between devices, to_row_before(): lax.ppermute(blocks, 'row', [(i, (i - 1) % rows_count) for i in range(row...  7.69 us
    all_to_all x1, starting transfers between devices, local(): lax.all_to_all(table_for_all(a_where, by_slot), both, split_axis=0, conca...  6.45 us
    all_to_all x1, starting transfers between devices, local(): lax.all_to_all(jnp.concatenate([a_send[0, 0], wrapped], axis=1), both, sp...  3.84 us
  transfers between devices with their start and end apart: 10, of which 4 were waited for; matrix products, arithmetic and copies ran while one was open for 7% of the time, Pallas kernels for 31%

profile of v1, /device:TPU:3, one launch (start us, length us, event | category | flops | bytes accessed | tf_op | source)
XLA Modules:
  0.0 144.2 jit_solution(7567225106319126693)
XLA Ops:
  0.0 1.6 %shard_map.46 = s32[32,2,128]{2,1,0:T(2,128)} custom-call(s32[2,1,32]{2,1,0:T(1,128)} %where_ref.1, s32[8,16]{1,0:T(8,128)} %bitcast.58), custom_call_target="tpu_custom_call" | custom-call | tf_op jit(solution)/shard_map/pallas_call | solution.py:567
  1.6 6.4 %all-to-all-start = ((s32[32,2,128]{2,1,0:T(2,128)}), s32[32,2,128]{2,1,0:T(2,128)S(1)}, u32[]{:S(2)}, u32[]{:S(2)}) async-start(s32[32,2,128]{2,1,0:T(2,128)} %shard_map.46), calls=%async_computation | async-start | bytes 65536 | tf_op jit(solution)/shard_map/all_to_all | solution.py:608
  8.0 1.7 %slice_bitcast_fusion = (bf16[32,128,128]{2,1,0:T(8,128)(2,1)S(1)}, bf16[1,1,32,128,128]{4,3,2,1,0:T(8,128)(2,1)S(1)}) fusion(bf16[2,1,32,128,128]{4,3,2,1,0:T(8,128)(2,1)} %param.10), kind=kLoop, calls=%fused_computation.1 | loop fusion | bytes 4194304 | tf_op jit(solution)/shard_map/squeeze | solution.py:639
  9.8 1.2 pad_maximum_fusion
  11.0 3.0 %all-to-all-done.tables = s32[32,2,128]{2,1,0:T(2,128)S(1)} async-done(((s32[32,2,128]{2,1,0:T(2,128)}), s32[32,2,128]{2,1,0:T(2,128)S(1)}, u32[]{:S(2)}, u32[]{:S(2)}) %all-to-all-start) | async-done | bytes 32800 | tf_op jit(solution)/shard_map/all_to_all | solution.py:608
  14.0 3.8 %all-to-all-start.1 = ((bf16[32,160,128]{2,1,0:T(8,128)(2,1)}), bf16[32,160,128]{2,1,0:T(8,128)(2,1)S(1)}, u32[]{:S(2)}, u32[]{:S(2)}) async-start(bf16[32,160,128]{2,1,0:T(8,128)(2,1)} %pad_maximum_fusion), calls=%async_computation.1 | async-start | bytes 2621440 | tf_op jit(solution)/shard_map/all_to_all | solution.py:638
  17.9 0.1 copy.34
  18.0 0.1 copy.37
  18.1 0.1 slice.93
  18.2 0.1 copy.39
  18.3 0.1 copy.38
  18.5 0.6 fusion.1
  19.1 0.2 fusion.3
  19.3 0.1 copy.40
  19.5 0.7 subtract_reduce_fusion
  20.1 0.1 copy.41
  20.2 0.7 fusion.5
  20.9 1.4 stack.32.spot
  22.3 6.6 %shard_map.48 = (bf16[16,128,128]{2,1,0:T(8,128)(2,1)}, bf16[16,128,128]{2,1,0:T(8,128)(2,1)}, bf16[8,128,128]{2,1,0:T(8,128)(2,1)}, bf16[8,128,128]{2,1,0:T(8,128)(2,1)}, bf16[24,128,128]{2,1,0:T(8,128)(2,1)}) custom-call(s32[7]{0:T(128)S(1)} %stack.32.spot, s32[32,2,128]{2,1,0:T(2,128)S(1)} %all-to-all-done.tables, bf16[128,128,128]{2,1,0:T(8,128)(2,1)} %bitcast.43), custom_call_target="tpu_custom_call" | custom-call | bytes 4718592 | tf_op jit(solution)/shard_map/pallas_call | solution.py:148
  28.9 0.4 collective-permute-start.7
  31.2 0.7 slice_bitcast_fusion.5.refs_0_
  31.9 0.7 slice_bitcast_fusion.3
  32.6 0.0 collective-permute-done.7.guests
  32.6 6.8 %shard_map.49 = (bf16[48,128,128]{2,1,0:T(8,128)(2,1)}, bf16[24,128,128]{2,1,0:T(8,128)(2,1)}) custom-call(s32[7]{0:T(128)S(1)} %stack.32.spot, s32[32,2,128]{2,1,0:T(2,128)S(1)} %all-to-all-done.tables, bf16[128,128,128]{2,1,0:T(8,128)(2,1)} %bitcast.44, bf16[16,128,128]{2,1,0:T(8,128)(2,1)S(1)} %collective-permute-done.7.guests, ...), custom_call_target="tpu_custom_call" | custom-call | bytes 4718592 | tf_op jit(solution)/shard_map/pallas_call | solution.py:148
  39.4 9.4 %all-to-all-done.1.received = bf16[32,160,128]{2,1,0:T(8,128)(2,1)S(1)} async-done(((bf16[32,160,128]{2,1,0:T(8,128)(2,1)}), bf16[32,160,128]{2,1,0:T(8,128)(2,1)S(1)}, u32[]{:S(2)}, u32[]{:S(2)}) %all-to-all-start.1) | async-done | bytes 1310752 | tf_op jit(solution)/shard_map/all_to_all | solution.py:638
  48.8 0.6 slice_bitcast_fusion.2.refs_2_
  49.4 2.8 %collective-permute-start.8 = (bf16[48,128,128]{2,1,0:T(8,128)(2,1)}, bf16[48,128,128]{2,1,0:T(8,128)(2,1)}, u32[]{:S(2)}, u32[]{:S(2)}) collective-permute-start(bf16[48,128,128]{2,1,0:T(8,128)(2,1)} %get-tuple-element.66), channel_id=1, source_target_pairs={{0,28},{4,0},{8,4},{12,8},{16,12},{20,16},{24,20},{28,24},{1,29},{... | collective-permute-start | bytes 4718600 | tf_op jit(solution)/shard_map/ppermute | solution.py:644
  52.2 0.7 collective-permute-start.3
  52.9 0.1 collective-permute-start.6
  53.1 1.3 collective-permute-start.5
  54.4 1.3 collective-permute-start.4
  55.7 41.4 %collective-permute-done.6.refs_4_ = bf16[16,128,128]{2,1,0:T(8,128)(2,1)S(1)} collective-permute-done((bf16[16,128,128]{2,1,0:T(8,128)(2,1)}, bf16[16,128,128]{2,1,0:T(8,128)(2,1)S(1)}, u32[]{:S(2)}, u32[]{:S(2)}) %collective-permute-start.6) | collective-permute-done | bytes 524320 | tf_op jit(solution)/shard_map/ppermute | solution.py:644
  97.1 0.8 copy-done
  97.9 4.8 %collective-permute-start.9 = (bf16[24,128,128]{2,1,0:T(8,128)(2,1)}, bf16[24,128,128]{2,1,0:T(8,128)(2,1)}, u32[]{:S(2)}, u32[]{:S(2)}) collective-permute-start(bf16[24,128,128]{2,1,0:T(8,128)(2,1)} %get-tuple-element.70), channel_id=1, source_target_pairs={{0,28},{4,0},{8,4},{12,8},{16,12},{20,16},{24,20},{28,24},{1,29},{... | collective-permute-start | bytes 2359304 | tf_op jit(solution)/shard_map/ppermute | solution.py:644
  102.7 1.3 pad_add_fusion.1.flags
  103.9 19.4 %shard_map.47 = (f32[2048,1024]{1,0:T(8,128)}, s32[32]{0:T(128)S(1)}, s32[19]{0:T(128)S(1)}, s32[128]{0:T(128)S(1)}) custom-call(s32[7]{0:T(128)S(1)} %stack.32.spot, s32[32,2,128]{2,1,0:T(2,128)S(1)} %all-to-all-done.tables, bf16[32,160,128]{2,1,0:T(8,128)(2,1)S(1)} %all-to-all-done.1.received, bf16[128,128,128]{2,1,0:T(8,128)(2,1)} %bitcast.45), custom_call_target="tpu_custom_call" | custom-call | flops 805306368 | bytes 16777216 | tf_op jit(solution)/shard_map/pallas_call | solution.py:512
  123.3 0.0 collective-permute-done.5.refs_2_
  123.3 0.0 collective-permute-done.4.refs_1_
  123.3 0.0 collective-permute-done.3.refs_0_
  123.3 0.0 collective-permute-done.8.refs_5_
  123.3 0.0 copy-done.1
  123.3 0.0 copy-start.2
  123.4 11.3 %shard_map.51 = (f32[2048,1024]{1,0:T(8,128)}, bf16[2048,1024]{1,0:T(8,128)(2,1)}, bf16[16,128,128]{2,1,0:T(8,128)(2,1)}, s32[16]{0:T(128)S(1)}, s32[16]{0:T(128)S(1)}) custom-call(s32[32]{0:T(128)S(1)} %get-tuple-element.56.order, s32[19]{0:T(128)S(1)} %get-tuple-element.57.first, s32[128]{0:T(128)S(1)} %get-tuple-element.58.target, ...), custom_call_target="tpu_custom_call" | custom-call | flops 536870912 | bytes 12582912 | tf_op jit(solution)/shard_map/pallas_call | solution.py:696
  134.7 2.5 %collective-permute-start.10 = (bf16[16,128,128]{2,1,0:T(8,128)(2,1)}, bf16[16,128,128]{2,1,0:T(8,128)(2,1)S(1)}, u32[]{:S(2)}, u32[]{:S(2)}) collective-permute-start(bf16[16,128,128]{2,1,0:T(8,128)(2,1)} %get-tuple-element.71), channel_id=1, source_target_pairs={{0,1},{1,0},{2,3},{3,2},{4,5},{5,4},{6,7},{7,6},{8,9},{9,8},{10,11... | collective-permute-start | bytes 1572872 | tf_op jit(solution)/shard_map/ppermute | solution.py:593
  137.2 0.0 collective-permute-done.9.refs_4_
  137.2 1.7 %collective-permute-done.10.refs_5_ = bf16[16,128,128]{2,1,0:T(8,128)(2,1)S(1)} collective-permute-done((bf16[16,128,128]{2,1,0:T(8,128)(2,1)}, bf16[16,128,128]{2,1,0:T(8,128)(2,1)S(1)}, u32[]{:S(2)}, u32[]{:S(2)}) %collective-permute-start.10) | collective-permute-done | bytes 524320 | tf_op jit(solution)/shard_map/ppermute | solution.py:593
  138.9 0.0 copy-done.2
  138.9 5.3 %shard_map.52 = bf16[2048,1024]{1,0:T(8,128)(2,1)} custom-call(s32[32]{0:T(128)S(1)} %get-tuple-element.56.order, s32[19]{0:T(128)S(1)} %get-tuple-element.57.first, s32[128]{0:T(128)S(1)} %get-tuple-element.58.target, s32[3]{0:T(128)S(1)} %pad_add_fusion.1.flags, s32[16]{0:T(128)S(1)} %get-tuple-element.68.touched, ...), custom_call_target="tpu_custom_call", output_to_operand_aliasing={{}: (16, {})} | custom-call | flops 536870912 | bytes 12582912 | tf_op jit(solution)/shard_map/pallas_call | solution.py:696
  (23 shorter events, 0.2 us)
Async XLA Ops:
  1.6 12.4 %all-to-all-start = ((s32[32,2,128]{2,1,0:T(2,128)}), s32[32,2,128]{2,1,0:T(2,128)S(1)}, u32[]{:S(2)}, u32[]{:S(2)}) async-start(s32[32,2,128]{2,1,0:T(2,128)} %shard_map.46), calls=%async_computation | async-start | bytes 65536 | tf_op jit(solution)/shard_map/all_to_all | solution.py:608
  14.0 34.8 %all-to-all-start.1 = ((bf16[32,160,128]{2,1,0:T(8,128)(2,1)}), bf16[32,160,128]{2,1,0:T(8,128)(2,1)S(1)}, u32[]{:S(2)}, u32[]{:S(2)}) async-start(bf16[32,160,128]{2,1,0:T(8,128)(2,1)} %pad_maximum_fusion), calls=%async_computation.1 | async-start | bytes 2621440 | tf_op jit(solution)/shard_map/all_to_all | solution.py:638
  28.9 3.7 %collective-permute-start.7 = (bf16[16,128,128]{2,1,0:T(8,128)(2,1)}, bf16[16,128,128]{2,1,0:T(8,128)(2,1)S(1)}, u32[]{:S(2)}, u32[]{:S(2)}) collective-permute-start(bf16[16,128,128]{2,1,0:T(8,128)(2,1)} %get-tuple-element.60), channel_id=1, source_target_pairs={{0,1},{1,0},{2,3},{3,2},{4,5},{5,4},{6,7},{7,6},{8,9},{9,8},{10,11... | collective-permute-start | bytes 1572872 | tf_op jit(solution)/shard_map/ppermute | solution.py:593
  49.4 73.9 %collective-permute-start.8 = (bf16[48,128,128]{2,1,0:T(8,128)(2,1)}, bf16[48,128,128]{2,1,0:T(8,128)(2,1)}, u32[]{:S(2)}, u32[]{:S(2)}) collective-permute-start(bf16[48,128,128]{2,1,0:T(8,128)(2,1)} %get-tuple-element.66), channel_id=1, source_target_pairs={{0,28},{4,0},{8,4},{12,8},{16,12},{20,16},{24,20},{28,24},{1,29},{... | collective-permute-start | bytes 4718600 | tf_op jit(solution)/shard_map/ppermute | solution.py:644
  52.2 71.1 %collective-permute-start.3 = (bf16[32,160,128]{2,1,0:T(8,128)(2,1)S(1)}, bf16[32,160,128]{2,1,0:T(8,128)(2,1)S(1)}, u32[]{:S(2)}, u32[]{:S(2)}) collective-permute-start(bf16[32,160,128]{2,1,0:T(8,128)(2,1)S(1)} %all-to-all-done.1.received), channel_id=1, source_target_pairs={{0,3},{1,0},{2,1},{3,2},{4,7},{5,4},{6,5},{7,6},{8,11},{9,8},{10,9... | collective-permute-start | bytes 3932168 | tf_op jit(solution)/shard_map/ppermute | solution.py:661
  52.9 44.2 %collective-permute-start.6 = (bf16[16,128,128]{2,1,0:T(8,128)(2,1)}, bf16[16,128,128]{2,1,0:T(8,128)(2,1)S(1)}, u32[]{:S(2)}, u32[]{:S(2)}) collective-permute-start(bf16[16,128,128]{2,1,0:T(8,128)(2,1)} %get-tuple-element.59), channel_id=1, source_target_pairs={{0,28},{4,0},{8,4},{12,8},{16,12},{20,16},{24,20},{28,24},{1,29},{... | collective-permute-start | bytes 1572872 | tf_op jit(solution)/shard_map/ppermute | solution.py:644
  53.1 70.2 %collective-permute-start.5 = (bf16[32,32,128]{2,1,0:T(8,128)(2,1)S(1)}, bf16[32,32,128]{2,1,0:T(8,128)(2,1)S(1)}, u32[]{:S(2)}, u32[]{:S(2)}) collective-permute-start(bf16[32,32,128]{2,1,0:T(8,128)(2,1)S(1)} %slice.96.refs_3_), channel_id=1, source_target_pairs={{2,3},{6,7},{10,11},{14,15},{18,19},{22,23},{26,27},{30,31}} | collective-permute-start | bytes 786440 | tf_op jit(solution)/shard_map/ppermute | solution.py:665
  54.4 68.9 %collective-permute-start.4 = (bf16[32,32,128]{2,1,0:T(8,128)(2,1)S(1)}, bf16[32,32,128]{2,1,0:T(8,128)(2,1)S(1)}, u32[]{:S(2)}, u32[]{:S(2)}) collective-permute-start(bf16[32,32,128]{2,1,0:T(8,128)(2,1)S(1)} %slice.96.refs_3_), channel_id=1, source_target_pairs={{1,3},{5,7},{9,11},{13,15},{17,19},{21,23},{25,27},{29,31}} | collective-permute-start | bytes 786440 | tf_op jit(solution)/shard_map/ppermute | solution.py:665
  97.1 0.8 copy-start
  97.9 39.3 %collective-permute-start.9 = (bf16[24,128,128]{2,1,0:T(8,128)(2,1)}, bf16[24,128,128]{2,1,0:T(8,128)(2,1)}, u32[]{:S(2)}, u32[]{:S(2)}) collective-permute-start(bf16[24,128,128]{2,1,0:T(8,128)(2,1)} %get-tuple-element.70), channel_id=1, source_target_pairs={{0,28},{4,0},{8,4},{12,8},{16,12},{20,16},{24,20},{28,24},{1,29},{... | collective-permute-start | bytes 2359304 | tf_op jit(solution)/shard_map/ppermute | solution.py:644
  103.9 19.4 %copy-start.1 = (bf16[16,128,128]{2,1,0:T(8,128)(2,1)S(1)}, bf16[16,128,128]{2,1,0:T(8,128)(2,1)}, u32[]{:S(2)}) copy-start(bf16[16,128,128]{2,1,0:T(8,128)(2,1)} %copy-done) | copy-start | bytes 1572868
  123.3 15.6 %copy-start.2 = (bf16[24,128,128]{2,1,0:T(8,128)(2,1)S(1)}, bf16[24,128,128]{2,1,0:T(8,128)(2,1)}, u32[]{:S(2)}) copy-start(bf16[24,128,128]{2,1,0:T(8,128)(2,1)} %get-tuple-element.86.refs_8_) | copy-start | bytes 2359300
  123.3 15.6 %copy-start.3 = (bf16[8,128,128]{2,1,0:T(8,128)(2,1)S(1)}, bf16[8,128,128]{2,1,0:T(8,128)(2,1)}, u32[]{:S(2)}) copy-start(bf16[8,128,128]{2,1,0:T(8,128)(2,1)} %get-tuple-element.85.refs_7_) | copy-start | bytes 786436
  123.4 15.5 %copy-start.4 = (bf16[8,128,128]{2,1,0:T(8,128)(2,1)S(1)}, bf16[8,128,128]{2,1,0:T(8,128)(2,1)}, u32[]{:S(2)}) copy-start(bf16[8,128,128]{2,1,0:T(8,128)(2,1)} %get-tuple-element.84.refs_6_) | copy-start | bytes 786436
  134.7 4.2 %collective-permute-start.10 = (bf16[16,128,128]{2,1,0:T(8,128)(2,1)}, bf16[16,128,128]{2,1,0:T(8,128)(2,1)S(1)}, u32[]{:S(2)}, u32[]{:S(2)}) collective-permute-start(bf16[16,128,128]{2,1,0:T(8,128)(2,1)} %get-tuple-element.71), channel_id=1, source_target_pairs={{0,1},{1,0},{2,3},{3,2},{4,5},{5,4},{6,7},{7,6},{8,9},{9,8},{10,11... | collective-permute-start | bytes 1572872 | tf_op jit(solution)/shard_map/ppermute | solution.py:593

commit v2 on v0

--- a/solution.py
+++ b/solution.py
@@ -169,6 +169,7 @@
         in_specs=[ANYWHERE] * (count + 1),
         out_specs=[ANYWHERE] * count,
         input_output_aliases={i: i for i in range(count)},
+        compiler_params=pltpu.CompilerParams(vmem_limit_bytes=LIMIT),
     )(*blocks, value)
 
 
@@ -216,6 +217,17 @@
     lax.fori_loop(low, KB, one, 0)
 
 
+def add_product(total, left, right, pair):
+    slot, column = pair // KB, pair % KB
+    wide = right.shape[-1]
+    step = 2 * left.shape[-1]
+    for low in range(0, wide, step):
+        here = pl.ds(low, step)
+        total[:, here] += jnp.dot(
+            left[slot], right[column, :, here], preferred_element_type=jnp.float32
+        )
+
+
 def add_rows(left, right, total, order, first):
     size = left.shape[1]
 
@@ -224,10 +236,7 @@
         here = pl.ds(pl.multiple_of(i * size, size), size)
 
         def add(entry, carry):
-            total[here, :] += jnp.dot(
-                left[order[entry] // KB], right[order[entry] % KB],
-                preferred_element_type=jnp.float32,
-            )
+            add_product(total.at[here], left, right, order[entry])
             return carry
 
         return lax.fori_loop(first[row], first[row + 1], add, carry)
@@ -325,10 +334,7 @@
     def add(entry, carry):
         @pl.when(touched[order[entry] % KB] > 0)
         def _():
-            total[row] += jnp.dot(
-                left[order[entry] // KB], right[order[entry] % KB],
-                preferred_element_type=jnp.float32,
-            )
+            add_product(total.at[row], left, right, order[entry])
 
         return carry
 
@@ -646,7 +652,7 @@
         pack_main, PARTS[:2], spot, tables, strips, swapped(guests),
         *(blocks[0, :16] for blocks in extra),
     )
-    early, late = map(to_row_before, after(received[0, :16], [early, late]))
+    early, late = map(to_row_before, after(received, [early, late]))
 
     shifted = lax.ppermute(
         received, "col", [(i, (i - 1) % cols_count) for i in range(cols_count)]

time: 121 us -> 121 us (level); the launches traced: 121 us -> 120 us
  no operation moved by 1% of the time
where the time goes in v2:
time: 121 us; the launch traced here: 120 us
  Pallas kernels  50.2 us (41%)
  waiting for transfers between devices  40.3 us (33%)
  starting transfers between devices  17.3 us (14%)
  local copies, waits for them, and re-layouts  5.85 us (5%)
  other arithmetic  4.12 us (3%)
  between operations  2.18 us (2%)
    ppermute x2, waiting for transfers between devices, to_row_before(): lax.ppermute(blocks, 'row', [(i, (i - 1) % rows_count) for i in range(row...  31 us
    pallas_call x1, Pallas kernels, step_call(): pl.pallas_call(kernel, out_shape=out_shape, grid_spec=pltpu.PrefetchScala...  20.2 us
    pallas_call x2, Pallas kernels, finish_call(): pl.pallas_call(kernel, out_shape=out_shape, grid_spec=pltpu.PrefetchScala...  15.9 us
    pallas_call x2, Pallas kernels, pack(): pl.pallas_call(kernel, out_shape=[pltpu.HBM((n, size, size), strips.dtype...  12.4 us
    all_to_all x1, waiting for transfers between devices, local(): lax.all_to_all(jnp.concatenate([a_send[0, 0], wrapped], axis=1), both, sp...  9.29 us
    all_to_all x1, starting transfers between devices, local(): lax.all_to_all(jnp.concatenate([a_send[0, 0], wrapped], axis=1), both, sp...  6.98 us
    all_to_all x1, starting transfers between devices, local(): lax.all_to_all(table_for_all(a_where, by_slot), both, split_axis=0, conca...  5.84 us
    ppermute x2, starting transfers between devices, local(): lax.ppermute(part, 'col', [(i, last)])  3.1 us
  transfers between devices with their start and end apart: 9, of which 3 were waited for; matrix products, arithmetic and copies ran while one was open for 8% of the time, Pallas kernels for 36%

profile of v2, /device:TPU:30, one launch (start us, length us, event | category | flops | bytes accessed | tf_op | source)
XLA Modules:
  0.0 120.0 jit_solution(13577447644673718204)
XLA Ops:
  0.0 1.6 %shard_map.46 = s32[32,2,128]{2,1,0:T(2,128)} custom-call(s32[2,1,32]{2,1,0:T(1,128)} %where_ref.1, s32[8,16]{1,0:T(8,128)} %bitcast.56), custom_call_target="tpu_custom_call" | custom-call | tf_op jit(solution)/shard_map/pallas_call | solution.py:564
  1.6 5.8 %all-to-all-start = ((s32[32,2,128]{2,1,0:T(2,128)}), s32[32,2,128]{2,1,0:T(2,128)S(1)}, u32[]{:S(2)}, u32[]{:S(2)}) async-start(s32[32,2,128]{2,1,0:T(2,128)} %shard_map.46), calls=%async_computation | async-start | bytes 65536 | tf_op jit(solution)/shard_map/all_to_all | solution.py:605
  7.4 1.7 %slice_bitcast_fusion = (bf16[32,128,128]{2,1,0:T(8,128)(2,1)S(1)}, bf16[1,1,32,128,128]{4,3,2,1,0:T(8,128)(2,1)S(1)}) fusion(bf16[2,1,32,128,128]{4,3,2,1,0:T(8,128)(2,1)} %param.10), kind=kLoop, calls=%fused_computation.1 | loop fusion | bytes 4194304 | tf_op jit(solution)/shard_map/squeeze | solution.py:636
  9.2 1.2 pad_maximum_fusion
  10.4 0.0 all-to-all-done.tables
  10.4 7.0 %all-to-all-start.1 = ((bf16[32,160,128]{2,1,0:T(8,128)(2,1)}), bf16[32,160,128]{2,1,0:T(8,128)(2,1)S(1)}, u32[]{:S(2)}, u32[]{:S(2)}) async-start(bf16[32,160,128]{2,1,0:T(8,128)(2,1)} %pad_maximum_fusion), calls=%async_computation.1 | async-start | bytes 2621440 | tf_op jit(solution)/shard_map/all_to_all | solution.py:635
  17.4 0.1 copy.34
  17.5 0.1 copy.37
  17.7 0.1 slice.89
  17.7 0.1 copy.39
  17.8 0.1 copy.38
  18.0 0.6 fusion.1
  18.6 0.2 fusion.3
  18.9 0.1 copy.40
  19.0 0.7 subtract_reduce_fusion
  19.7 0.1 copy.41
  19.8 0.7 fusion.5
  20.4 1.4 %stack.32.spot = s32[7]{0:T(128)S(1)} concatenate(s32[1]{0:T(128)} %bitcast, s32[1]{0:T(128)} %bitcast.1, s32[1]{0:T(128)} %bitcast.2, s32[1]{0:T(128)} %bitcast.3, s32[1]{0:T(128)} %bitcast.4, s32[1]{0:T(128)} %bitcast.17, s32[1]{0:T(128)} %bitcast.18), dimensions={0} | concatenate | bytes 56 | tf_op jit(solution)/shard_map/stack | solution.py:623
  21.8 5.8 %shard_map.48 = (bf16[16,128,128]{2,1,0:T(8,128)(2,1)}, bf16[8,128,128]{2,1,0:T(8,128)(2,1)}, bf16[8,128,128]{2,1,0:T(8,128)(2,1)}, bf16[24,128,128]{2,1,0:T(8,128)(2,1)}) custom-call(s32[7]{0:T(128)S(1)} %stack.32.spot, s32[32,2,128]{2,1,0:T(2,128)S(1)} %all-to-all-done.tables, bf16[128,128,128]{2,1,0:T(8,128)(2,1)} %bitcast.41), custom_call_target="tpu_custom_call" | custom-call | bytes 3670016 | tf_op jit(solution)/shard_map/pallas_call | solution.py:140
  27.6 0.2 collective-permute-start.6
  29.8 0.7 slice_bitcast_fusion.4.refs_0_
  30.5 0.7 slice_bitcast_fusion.2
  31.2 0.0 collective-permute-done.6.guests
  31.2 6.6 %shard_map.49 = (bf16[64,128,128]{2,1,0:T(8,128)(2,1)}, bf16[24,128,128]{2,1,0:T(8,128)(2,1)}) custom-call(s32[7]{0:T(128)S(1)} %stack.32.spot, s32[32,2,128]{2,1,0:T(2,128)S(1)} %all-to-all-done.tables, bf16[128,128,128]{2,1,0:T(8,128)(2,1)} %bitcast.42, bf16[16,128,128]{2,1,0:T(8,128)(2,1)S(1)} %collective-permute-done.6.guests, ...), custom_call_target="tpu_custom_call" | custom-call | bytes 5767168 | tf_op jit(solution)/shard_map/pallas_call | solution.py:140
  37.8 9.3 %all-to-all-done.1.received.refs_2_ = bf16[32,160,128]{2,1,0:T(8,128)(2,1)S(1)} async-done(((bf16[32,160,128]{2,1,0:T(8,128)(2,1)}), bf16[32,160,128]{2,1,0:T(8,128)(2,1)S(1)}, u32[]{:S(2)}, u32[]{:S(2)}) %all-to-all-start.1) | async-done | bytes 1310752 | tf_op jit(solution)/shard_map/all_to_all | solution.py:635
  47.1 0.4 collective-permute-start.7
  47.5 0.0 collective-permute-start.3
  47.5 2.4 %collective-permute-start.5 = (bf16[32,32,128]{2,1,0:T(8,128)(2,1)S(1)}, bf16[32,32,128]{2,1,0:T(8,128)(2,1)S(1)}, u32[]{:S(2)}, u32[]{:S(2)}) collective-permute-start(bf16[32,32,128]{2,1,0:T(8,128)(2,1)S(1)} %slice.92.refs_3_), channel_id=1, source_target_pairs={{2,3},{6,7},{10,11},{14,15},{18,19},{22,23},{26,27},{30,31}} | collective-permute-start | bytes 786440 | tf_op jit(solution)/shard_map/ppermute | solution.py:661
  50.0 0.7 collective-permute-start.4
  50.6 0.7 collective-permute-start.8
  51.3 1.3 %pad_add_fusion.1.flags = s32[3]{0:T(128)S(1)} fusion(s32[1]{0:T(128)} %bitcast.25, s32[1]{0:T(128)} %bitcast.24, s32[1]{0:T(128)} %bitcast.23), kind=kLoop, calls=%fused_computation.22 | loop fusion | flops 6 | bytes 24 | tf_op jit(solution)/shard_map/stack | solution.py:688
  52.6 20.2 %shard_map.47 = (f32[2048,1024]{1,0:T(8,128)}, s32[32]{0:T(128)S(1)}, s32[19]{0:T(128)S(1)}, s32[128]{0:T(128)S(1)}) custom-call(s32[7]{0:T(128)S(1)} %stack.32.spot, s32[32,2,128]{2,1,0:T(2,128)S(1)} %all-to-all-done.tables, bf16[32,160,128]{2,1,0:T(8,128)(2,1)S(1)} %all-to-all-done.1.received.refs_2_, bf16[128,128,128]{2,1,0:T(8,128)(2,1)} %bitcast.43), custom_call_target="tpu_custom_call" | custom-call | flops 805306368 | bytes 16777216 | tf_op jit(solution)/shard_map/pallas_call | solution.py:509
  72.9 0.0 collective-permute-done.5.refs_2_
  72.9 0.0 collective-permute-done.4.refs_1_
  72.9 0.0 collective-permute-done.3.refs_0_
  72.9 25.7 %collective-permute-done.7.refs_4_ = bf16[64,128,128]{2,1,0:T(8,128)(2,1)} collective-permute-done((bf16[64,128,128]{2,1,0:T(8,128)(2,1)}, bf16[64,128,128]{2,1,0:T(8,128)(2,1)}, u32[]{:S(2)}, u32[]{:S(2)}) %collective-permute-start.7) | collective-permute-done | bytes 2097184 | tf_op jit(solution)/shard_map/ppermute | solution.py:641
  98.6 0.0 copy-start
  98.6 0.0 copy-start.1
  98.6 0.0 copy-start.2
  98.6 10.5 %shard_map.51 = (f32[2048,1024]{1,0:T(8,128)}, bf16[2048,1024]{1,0:T(8,128)(2,1)}, bf16[16,128,128]{2,1,0:T(8,128)(2,1)}, s32[16]{0:T(128)S(1)}, s32[16]{0:T(128)S(1)}) custom-call(s32[32]{0:T(128)S(1)} %get-tuple-element.55.order, s32[19]{0:T(128)S(1)} %get-tuple-element.56.first, s32[128]{0:T(128)S(1)} %get-tuple-element.57.target, ...), custom_call_target="tpu_custom_call" | custom-call | flops 536870912 | bytes 12582912 | tf_op jit(solution)/shard_map/pallas_call | solution.py:692
  109.2 0.1 collective-permute-start.9
  109.2 5.3 %collective-permute-done.8.refs_4_ = bf16[24,128,128]{2,1,0:T(8,128)(2,1)} collective-permute-done((bf16[24,128,128]{2,1,0:T(8,128)(2,1)}, bf16[24,128,128]{2,1,0:T(8,128)(2,1)}, u32[]{:S(2)}, u32[]{:S(2)}) %collective-permute-start.8) | collective-permute-done | bytes 786464 | tf_op jit(solution)/shard_map/ppermute | solution.py:641
  114.6 0.0 collective-permute-done.9.refs_5_
  114.6 0.0 copy-done
  114.6 0.0 copy-done.1
  114.6 0.0 copy-done.2
  114.6 5.4 %shard_map.52 = bf16[2048,1024]{1,0:T(8,128)(2,1)} custom-call(s32[32]{0:T(128)S(1)} %get-tuple-element.55.order, s32[19]{0:T(128)S(1)} %get-tuple-element.56.first, s32[128]{0:T(128)S(1)} %get-tuple-element.57.target, s32[3]{0:T(128)S(1)} %pad_add_fusion.1.flags, s32[16]{0:T(128)S(1)} %get-tuple-element.66.touched, ...), custom_call_target="tpu_custom_call", output_to_operand_aliasing={{}: (16, {})} | custom-call | flops 536870912 | bytes 12582912 | tf_op jit(solution)/shard_map/pallas_call | solution.py:692
  (17 shorter events, 0.2 us)
Async XLA Ops:
  1.6 8.8 %all-to-all-start = ((s32[32,2,128]{2,1,0:T(2,128)}), s32[32,2,128]{2,1,0:T(2,128)S(1)}, u32[]{:S(2)}, u32[]{:S(2)}) async-start(s32[32,2,128]{2,1,0:T(2,128)} %shard_map.46), calls=%async_computation | async-start | bytes 65536 | tf_op jit(solution)/shard_map/all_to_all | solution.py:605
  10.4 36.7 %all-to-all-start.1 = ((bf16[32,160,128]{2,1,0:T(8,128)(2,1)}), bf16[32,160,128]{2,1,0:T(8,128)(2,1)S(1)}, u32[]{:S(2)}, u32[]{:S(2)}) async-start(bf16[32,160,128]{2,1,0:T(8,128)(2,1)} %pad_maximum_fusion), calls=%async_computation.1 | async-start | bytes 2621440 | tf_op jit(solution)/shard_map/all_to_all | solution.py:635
  27.6 3.5 %collective-permute-start.6 = (bf16[16,128,128]{2,1,0:T(8,128)(2,1)}, bf16[16,128,128]{2,1,0:T(8,128)(2,1)S(1)}, u32[]{:S(2)}, u32[]{:S(2)}) collective-permute-start(bf16[16,128,128]{2,1,0:T(8,128)(2,1)} %get-tuple-element.58), channel_id=1, source_target_pairs={{0,1},{1,0},{2,3},{3,2},{4,5},{5,4},{6,7},{7,6},{8,9},{9,8},{10,11... | collective-permute-start | bytes 1572872 | tf_op jit(solution)/shard_map/ppermute | solution.py:590
  47.1 51.5 %collective-permute-start.7 = (bf16[64,128,128]{2,1,0:T(8,128)(2,1)}, bf16[64,128,128]{2,1,0:T(8,128)(2,1)}, u32[]{:S(2)}, u32[]{:S(2)}) collective-permute-start(bf16[64,128,128]{2,1,0:T(8,128)(2,1)} %get-tuple-element.64), channel_id=1, source_target_pairs={{0,28},{4,0},{8,4},{12,8},{16,12},{20,16},{24,20},{28,24},{1,29},{... | collective-permute-start | bytes 6291464 | tf_op jit(solution)/shard_map/ppermute | solution.py:641
  47.5 25.4 %collective-permute-start.3 = (bf16[32,160,128]{2,1,0:T(8,128)(2,1)S(1)}, bf16[32,160,128]{2,1,0:T(8,128)(2,1)S(1)}, u32[]{:S(2)}, u32[]{:S(2)}) collective-permute-start(bf16[32,160,128]{2,1,0:T(8,128)(2,1)S(1)} %all-to-all-done.1.received.refs_2_), channel_id=1, source_target_pairs={{0,3},{1,0},{2,1},{3,2},{4,7},{5,4},{6,5},{7,6},{8,11},{9,8},{10,9... | collective-permute-start | bytes 3932168 | tf_op jit(solution)/shard_map/ppermute | solution.py:657
  47.5 25.4 %collective-permute-start.5 = (bf16[32,32,128]{2,1,0:T(8,128)(2,1)S(1)}, bf16[32,32,128]{2,1,0:T(8,128)(2,1)S(1)}, u32[]{:S(2)}, u32[]{:S(2)}) collective-permute-start(bf16[32,32,128]{2,1,0:T(8,128)(2,1)S(1)} %slice.92.refs_3_), channel_id=1, source_target_pairs={{2,3},{6,7},{10,11},{14,15},{18,19},{22,23},{26,27},{30,31}} | collective-permute-start | bytes 786440 | tf_op jit(solution)/shard_map/ppermute | solution.py:661
  50.0 23.0 %collective-permute-start.4 = (bf16[32,32,128]{2,1,0:T(8,128)(2,1)S(1)}, bf16[32,32,128]{2,1,0:T(8,128)(2,1)S(1)}, u32[]{:S(2)}, u32[]{:S(2)}) collective-permute-start(bf16[32,32,128]{2,1,0:T(8,128)(2,1)S(1)} %slice.92.refs_3_), channel_id=1, source_target_pairs={{1,3},{5,7},{9,11},{13,15},{17,19},{21,23},{25,27},{29,31}} | collective-permute-start | bytes 786440 | tf_op jit(solution)/shard_map/ppermute | solution.py:661
  50.6 63.9 %collective-permute-start.8 = (bf16[24,128,128]{2,1,0:T(8,128)(2,1)}, bf16[24,128,128]{2,1,0:T(8,128)(2,1)}, u32[]{:S(2)}, u32[]{:S(2)}) collective-permute-start(bf16[24,128,128]{2,1,0:T(8,128)(2,1)} %get-tuple-element.68), channel_id=1, source_target_pairs={{0,28},{4,0},{8,4},{12,8},{16,12},{20,16},{24,20},{28,24},{1,29},{... | collective-permute-start | bytes 2359304 | tf_op jit(solution)/shard_map/ppermute | solution.py:641
  98.6 16.0 %copy-start = (bf16[24,128,128]{2,1,0:T(8,128)(2,1)S(1)}, bf16[24,128,128]{2,1,0:T(8,128)(2,1)}, u32[]{:S(2)}) copy-start(bf16[24,128,128]{2,1,0:T(8,128)(2,1)} %get-tuple-element.84.refs_8_) | copy-start | bytes 2359300
  98.6 16.0 %copy-start.1 = (bf16[8,128,128]{2,1,0:T(8,128)(2,1)S(1)}, bf16[8,128,128]{2,1,0:T(8,128)(2,1)}, u32[]{:S(2)}) copy-start(bf16[8,128,128]{2,1,0:T(8,128)(2,1)} %get-tuple-element.83.refs_7_) | copy-start | bytes 786436
  98.6 16.0 %copy-start.2 = (bf16[8,128,128]{2,1,0:T(8,128)(2,1)S(1)}, bf16[8,128,128]{2,1,0:T(8,128)(2,1)}, u32[]{:S(2)}) copy-start(bf16[8,128,128]{2,1,0:T(8,128)(2,1)} %get-tuple-element.82.refs_6_) | copy-start | bytes 786436
  109.2 5.4 %collective-permute-start.9 = (bf16[16,128,128]{2,1,0:T(8,128)(2,1)}, bf16[16,128,128]{2,1,0:T(8,128)(2,1)S(1)}, u32[]{:S(2)}, u32[]{:S(2)}) collective-permute-start(bf16[16,128,128]{2,1,0:T(8,128)(2,1)} %get-tuple-element.69), channel_id=1, source_target_pairs={{0,1},{1,0},{2,3},{3,2},{4,5},{5,4},{6,7},{7,6},{8,9},{9,8},{10,11... | collective-permute-start | bytes 1572872 | tf_op jit(solution)/shard_map/ppermute | solution.py:590

commit v3 on v2

--- a/solution.py
+++ b/solution.py
@@ -10,7 +10,7 @@
 RB = 16
 KB = 16
 NJ = 8
-PARTS = (64, 24, 8, 8, 24)
+PARTS = (70, 22, 8, 8, 20)
 ALWAYS = PARTS[0] + PARTS[1]
 LENT = 16
 GROUP = 4

time: 121 us -> 122 us (level)
  waiting for transfers between devices: 40.3 us -> 42 us
    ppermute x2, waiting for transfers between devices: 31 us -> 32.7 us  [to_row_before(): lax.ppermute(blocks, 'row', [(i, (i - 1) % rows_count) for i in range(row...]
    pallas_call x2, Pallas kernels: 15.9 us -> 14.5 us  [finish_call(): pl.pallas_call(kernel, out_shape=out_shape, grid_spec=pltpu.PrefetchScala...]
  transfers between devices with their start and end apart: 9 -> 9, of which waited for: 3 -> 3; matrix products, arithmetic and copies ran while one was open for 8% -> 8% of each run, Pallas kernels for 36% -> 37%
where the time goes in v3:
time: 122 us; the launch traced here: 120 us
  Pallas kernels  49.2 us (40%)
  waiting for transfers between devices  42 us (34%)
  starting transfers between devices  17.3 us (14%)
  local copies, waits for them, and re-layouts  5.85 us (5%)
  other arithmetic  4.08 us (3%)
  between operations  1.98 us (2%)
    ppermute x2, waiting for transfers between devices, to_row_before(): lax.ppermute(blocks, 'row', [(i, (i - 1) % rows_count) for i in range(row...  32.7 us
    pallas_call x1, Pallas kernels, step_call(): pl.pallas_call(kernel, out_shape=out_shape, grid_spec=pltpu.PrefetchScala...  20.5 us
    pallas_call x2, Pallas kernels, finish_call(): pl.pallas_call(kernel, out_shape=out_shape, grid_spec=pltpu.PrefetchScala...  14.5 us
    pallas_call x2, Pallas kernels, pack(): pl.pallas_call(kernel, out_shape=[pltpu.HBM((n, size, size), strips.dtype...  12.7 us
    all_to_all x1, waiting for transfers between devices, local(): lax.all_to_all(jnp.concatenate([a_send[0, 0], wrapped], axis=1), both, sp...  9.24 us
    all_to_all x1, starting transfers between devices, local(): lax.all_to_all(jnp.concatenate([a_send[0, 0], wrapped], axis=1), both, sp...  6.98 us
    all_to_all x1, starting transfers between devices, local(): lax.all_to_all(table_for_all(a_where, by_slot), both, split_axis=0, conca...  5.84 us
    ppermute x2, starting transfers between devices, local(): lax.ppermute(part, 'col', [(i, last)])  3.1 us
  transfers between devices with their start and end apart: 9, of which 3 were waited for; matrix products, arithmetic and copies ran while one was open for 8% of the time, Pallas kernels for 37%

profile of v3, /device:TPU:30, one launch (start us, length us, event | category | flops | bytes accessed | tf_op | source)
XLA Modules:
  0.0 120.5 jit_solution(10332604961557052220)
XLA Ops:
  0.0 1.6 %shard_map.46 = s32[32,2,128]{2,1,0:T(2,128)} custom-call(s32[2,1,32]{2,1,0:T(1,128)} %where_ref.1, s32[8,16]{1,0:T(8,128)} %bitcast.56), custom_call_target="tpu_custom_call" | custom-call | tf_op jit(solution)/shard_map/pallas_call | solution.py:564
  1.6 5.8 %all-to-all-start = ((s32[32,2,128]{2,1,0:T(2,128)}), s32[32,2,128]{2,1,0:T(2,128)S(1)}, u32[]{:S(2)}, u32[]{:S(2)}) async-start(s32[32,2,128]{2,1,0:T(2,128)} %shard_map.46), calls=%async_computation | async-start | bytes 65536 | tf_op jit(solution)/shard_map/all_to_all | solution.py:605
  7.4 1.7 %slice_bitcast_fusion = (bf16[32,128,128]{2,1,0:T(8,128)(2,1)S(1)}, bf16[1,1,32,128,128]{4,3,2,1,0:T(8,128)(2,1)S(1)}) fusion(bf16[2,1,32,128,128]{4,3,2,1,0:T(8,128)(2,1)} %param.10), kind=kLoop, calls=%fused_computation.1 | loop fusion | bytes 4194304 | tf_op jit(solution)/shard_map/squeeze | solution.py:636
  9.2 1.2 pad_maximum_fusion
  10.4 0.0 all-to-all-done.tables
  10.4 7.0 %all-to-all-start.1 = ((bf16[32,160,128]{2,1,0:T(8,128)(2,1)}), bf16[32,160,128]{2,1,0:T(8,128)(2,1)S(1)}, u32[]{:S(2)}, u32[]{:S(2)}) async-start(bf16[32,160,128]{2,1,0:T(8,128)(2,1)} %pad_maximum_fusion), calls=%async_computation.1 | async-start | bytes 2621440 | tf_op jit(solution)/shard_map/all_to_all | solution.py:635
  17.4 0.1 copy.34
  17.5 0.1 copy.37
  17.7 0.1 slice.89
  17.7 0.1 copy.39
  17.8 0.1 copy.38
  18.0 0.6 fusion.1
  18.6 0.2 fusion.3
  18.9 0.1 copy.40
  19.0 0.6 subtract_reduce_fusion
  19.6 0.1 copy.41
  19.7 0.7 fusion.5
  20.4 1.4 %stack.32.spot = s32[7]{0:T(128)S(1)} concatenate(s32[1]{0:T(128)} %bitcast, s32[1]{0:T(128)} %bitcast.1, s32[1]{0:T(128)} %bitcast.2, s32[1]{0:T(128)} %bitcast.3, s32[1]{0:T(128)} %bitcast.4, s32[1]{0:T(128)} %bitcast.17, s32[1]{0:T(128)} %bitcast.18), dimensions={0} | concatenate | bytes 56 | tf_op jit(solution)/shard_map/stack | solution.py:623
  21.8 5.7 %shard_map.48 = (bf16[16,128,128]{2,1,0:T(8,128)(2,1)}, bf16[8,128,128]{2,1,0:T(8,128)(2,1)}, bf16[8,128,128]{2,1,0:T(8,128)(2,1)}, bf16[20,128,128]{2,1,0:T(8,128)(2,1)}) custom-call(s32[7]{0:T(128)S(1)} %stack.32.spot, s32[32,2,128]{2,1,0:T(2,128)S(1)} %all-to-all-done.tables, bf16[128,128,128]{2,1,0:T(8,128)(2,1)} %bitcast.41), custom_call_target="tpu_custom_call" | custom-call | bytes 3407872 | tf_op jit(solution)/shard_map/pallas_call | solution.py:140
  27.5 0.2 collective-permute-start.6
  29.5 0.7 slice_bitcast_fusion.4.refs_0_
  30.2 0.7 slice_bitcast_fusion.2
  30.9 0.0 collective-permute-done.6.guests
  30.9 7.0 %shard_map.49 = (bf16[70,128,128]{2,1,0:T(8,128)(2,1)}, bf16[22,128,128]{2,1,0:T(8,128)(2,1)}) custom-call(s32[7]{0:T(128)S(1)} %stack.32.spot, s32[32,2,128]{2,1,0:T(2,128)S(1)} %all-to-all-done.tables, bf16[128,128,128]{2,1,0:T(8,128)(2,1)} %bitcast.42, bf16[16,128,128]{2,1,0:T(8,128)(2,1)S(1)} %collective-permute-done.6.guests, ...), custom_call_target="tpu_custom_call" | custom-call | bytes 6029312 | tf_op jit(solution)/shard_map/pallas_call | solution.py:140
  37.9 9.2 %all-to-all-done.1.received.refs_2_ = bf16[32,160,128]{2,1,0:T(8,128)(2,1)S(1)} async-done(((bf16[32,160,128]{2,1,0:T(8,128)(2,1)}), bf16[32,160,128]{2,1,0:T(8,128)(2,1)S(1)}, u32[]{:S(2)}, u32[]{:S(2)}) %all-to-all-start.1) | async-done | bytes 1310752 | tf_op jit(solution)/shard_map/all_to_all | solution.py:635
  47.1 0.4 collective-permute-start.7
  47.5 0.0 collective-permute-start.3
  47.5 2.4 %collective-permute-start.5 = (bf16[32,32,128]{2,1,0:T(8,128)(2,1)S(1)}, bf16[32,32,128]{2,1,0:T(8,128)(2,1)S(1)}, u32[]{:S(2)}, u32[]{:S(2)}) collective-permute-start(bf16[32,32,128]{2,1,0:T(8,128)(2,1)S(1)} %slice.92.refs_3_), channel_id=1, source_target_pairs={{2,3},{6,7},{10,11},{14,15},{18,19},{22,23},{26,27},{30,31}} | collective-permute-start | bytes 786440 | tf_op jit(solution)/shard_map/ppermute | solution.py:661
  50.0 0.7 collective-permute-start.4
  50.6 0.7 collective-permute-start.8
  51.3 1.3 %pad_add_fusion.1.flags = s32[3]{0:T(128)S(1)} fusion(s32[1]{0:T(128)} %bitcast.25, s32[1]{0:T(128)} %bitcast.24, s32[1]{0:T(128)} %bitcast.23), kind=kLoop, calls=%fused_computation.22 | loop fusion | flops 6 | bytes 24 | tf_op jit(solution)/shard_map/stack | solution.py:688
  52.7 20.5 %shard_map.47 = (f32[2048,1024]{1,0:T(8,128)}, s32[32]{0:T(128)S(1)}, s32[19]{0:T(128)S(1)}, s32[128]{0:T(128)S(1)}) custom-call(s32[7]{0:T(128)S(1)} %stack.32.spot, s32[32,2,128]{2,1,0:T(2,128)S(1)} %all-to-all-done.tables, bf16[32,160,128]{2,1,0:T(8,128)(2,1)S(1)} %all-to-all-done.1.received.refs_2_, bf16[128,128,128]{2,1,0:T(8,128)(2,1)} %bitcast.43), custom_call_target="tpu_custom_call" | custom-call | flops 805306368 | bytes 16777216 | tf_op jit(solution)/shard_map/pallas_call | solution.py:509
  73.1 0.0 collective-permute-done.5.refs_2_
  73.2 0.0 collective-permute-done.4.refs_1_
  73.2 0.0 collective-permute-done.3.refs_0_
  73.2 29.6 %collective-permute-done.7.refs_4_ = bf16[70,128,128]{2,1,0:T(8,128)(2,1)} collective-permute-done((bf16[70,128,128]{2,1,0:T(8,128)(2,1)}, bf16[70,128,128]{2,1,0:T(8,128)(2,1)}, u32[]{:S(2)}, u32[]{:S(2)}) %collective-permute-start.7) | collective-permute-done | bytes 2293792 | tf_op jit(solution)/shard_map/ppermute | solution.py:641
  102.8 0.0 copy-start
  102.8 0.0 copy-start.1
  102.8 0.0 copy-start.2
  102.8 11.3 %shard_map.51 = (f32[2048,1024]{1,0:T(8,128)}, bf16[2048,1024]{1,0:T(8,128)(2,1)}, bf16[16,128,128]{2,1,0:T(8,128)(2,1)}, s32[16]{0:T(128)S(1)}, s32[16]{0:T(128)S(1)}) custom-call(s32[32]{0:T(128)S(1)} %get-tuple-element.55.order, s32[19]{0:T(128)S(1)} %get-tuple-element.56.first, s32[128]{0:T(128)S(1)} %get-tuple-element.57.target, ...), custom_call_target="tpu_custom_call" | custom-call | flops 536870912 | bytes 12582912 | tf_op jit(solution)/shard_map/pallas_call | solution.py:692
  114.1 0.1 collective-permute-start.9
  114.2 3.1 %collective-permute-done.8.refs_4_ = bf16[22,128,128]{2,1,0:T(8,128)(2,1)S(1)} collective-permute-done((bf16[22,128,128]{2,1,0:T(8,128)(2,1)}, bf16[22,128,128]{2,1,0:T(8,128)(2,1)S(1)}, u32[]{:S(2)}, u32[]{:S(2)}) %collective-permute-start.8) | collective-permute-done | bytes 720928 | tf_op jit(solution)/shard_map/ppermute | solution.py:641
  117.3 0.0 collective-permute-done.9.refs_5_
  117.3 0.0 copy-done
  117.3 0.0 copy-done.1
  117.3 0.0 copy-done.2
  117.3 3.2 %shard_map.52 = bf16[2048,1024]{1,0:T(8,128)(2,1)} custom-call(s32[32]{0:T(128)S(1)} %get-tuple-element.55.order, s32[19]{0:T(128)S(1)} %get-tuple-element.56.first, s32[128]{0:T(128)S(1)} %get-tuple-element.57.target, s32[3]{0:T(128)S(1)} %pad_add_fusion.1.flags, s32[16]{0:T(128)S(1)} %get-tuple-element.66.touched, ...), custom_call_target="tpu_custom_call", output_to_operand_aliasing={{}: (16, {})} | custom-call | flops 536870912 | bytes 12582912 | tf_op jit(solution)/shard_map/pallas_call | solution.py:692
  (17 shorter events, 0.2 us)
Async XLA Ops:
  1.6 8.8 %all-to-all-start = ((s32[32,2,128]{2,1,0:T(2,128)}), s32[32,2,128]{2,1,0:T(2,128)S(1)}, u32[]{:S(2)}, u32[]{:S(2)}) async-start(s32[32,2,128]{2,1,0:T(2,128)} %shard_map.46), calls=%async_computation | async-start | bytes 65536 | tf_op jit(solution)/shard_map/all_to_all | solution.py:605
  10.4 36.7 %all-to-all-start.1 = ((bf16[32,160,128]{2,1,0:T(8,128)(2,1)}), bf16[32,160,128]{2,1,0:T(8,128)(2,1)S(1)}, u32[]{:S(2)}, u32[]{:S(2)}) async-start(bf16[32,160,128]{2,1,0:T(8,128)(2,1)} %pad_maximum_fusion), calls=%async_computation.1 | async-start | bytes 2621440 | tf_op jit(solution)/shard_map/all_to_all | solution.py:635
  27.5 3.3 %collective-permute-start.6 = (bf16[16,128,128]{2,1,0:T(8,128)(2,1)}, bf16[16,128,128]{2,1,0:T(8,128)(2,1)S(1)}, u32[]{:S(2)}, u32[]{:S(2)}) collective-permute-start(bf16[16,128,128]{2,1,0:T(8,128)(2,1)} %get-tuple-element.58), channel_id=1, source_target_pairs={{0,1},{1,0},{2,3},{3,2},{4,5},{5,4},{6,7},{7,6},{8,9},{9,8},{10,11... | collective-permute-start | bytes 1572872 | tf_op jit(solution)/shard_map/ppermute | solution.py:590
  47.1 55.7 %collective-permute-start.7 = (bf16[70,128,128]{2,1,0:T(8,128)(2,1)}, bf16[70,128,128]{2,1,0:T(8,128)(2,1)}, u32[]{:S(2)}, u32[]{:S(2)}) collective-permute-start(bf16[70,128,128]{2,1,0:T(8,128)(2,1)} %get-tuple-element.64), channel_id=1, source_target_pairs={{0,28},{4,0},{8,4},{12,8},{16,12},{20,16},{24,20},{28,24},{1,29},{... | collective-permute-start | bytes 6881288 | tf_op jit(solution)/shard_map/ppermute | solution.py:641
  47.5 25.7 %collective-permute-start.3 = (bf16[32,160,128]{2,1,0:T(8,128)(2,1)S(1)}, bf16[32,160,128]{2,1,0:T(8,128)(2,1)S(1)}, u32[]{:S(2)}, u32[]{:S(2)}) collective-permute-start(bf16[32,160,128]{2,1,0:T(8,128)(2,1)S(1)} %all-to-all-done.1.received.refs_2_), channel_id=1, source_target_pairs={{0,3},{1,0},{2,1},{3,2},{4,7},{5,4},{6,5},{7,6},{8,11},{9,8},{10,9... | collective-permute-start | bytes 3932168 | tf_op jit(solution)/shard_map/ppermute | solution.py:657
  47.5 25.6 %collective-permute-start.5 = (bf16[32,32,128]{2,1,0:T(8,128)(2,1)S(1)}, bf16[32,32,128]{2,1,0:T(8,128)(2,1)S(1)}, u32[]{:S(2)}, u32[]{:S(2)}) collective-permute-start(bf16[32,32,128]{2,1,0:T(8,128)(2,1)S(1)} %slice.92.refs_3_), channel_id=1, source_target_pairs={{2,3},{6,7},{10,11},{14,15},{18,19},{22,23},{26,27},{30,31}} | collective-permute-start | bytes 786440 | tf_op jit(solution)/shard_map/ppermute | solution.py:661
  50.0 23.2 %collective-permute-start.4 = (bf16[32,32,128]{2,1,0:T(8,128)(2,1)S(1)}, bf16[32,32,128]{2,1,0:T(8,128)(2,1)S(1)}, u32[]{:S(2)}, u32[]{:S(2)}) collective-permute-start(bf16[32,32,128]{2,1,0:T(8,128)(2,1)S(1)} %slice.92.refs_3_), channel_id=1, source_target_pairs={{1,3},{5,7},{9,11},{13,15},{17,19},{21,23},{25,27},{29,31}} | collective-permute-start | bytes 786440 | tf_op jit(solution)/shard_map/ppermute | solution.py:661
  50.6 66.6 %collective-permute-start.8 = (bf16[22,128,128]{2,1,0:T(8,128)(2,1)}, bf16[22,128,128]{2,1,0:T(8,128)(2,1)S(1)}, u32[]{:S(2)}, u32[]{:S(2)}) collective-permute-start(bf16[22,128,128]{2,1,0:T(8,128)(2,1)} %get-tuple-element.68), channel_id=1, source_target_pairs={{0,28},{4,0},{8,4},{12,8},{16,12},{20,16},{24,20},{28,24},{1,29},{... | collective-permute-start | bytes 2162696 | tf_op jit(solution)/shard_map/ppermute | solution.py:641
  102.8 14.5 %copy-start = (bf16[20,128,128]{2,1,0:T(8,128)(2,1)S(1)}, bf16[20,128,128]{2,1,0:T(8,128)(2,1)}, u32[]{:S(2)}) copy-start(bf16[20,128,128]{2,1,0:T(8,128)(2,1)} %get-tuple-element.84.refs_8_) | copy-start | bytes 1966084
  102.8 14.5 %copy-start.1 = (bf16[8,128,128]{2,1,0:T(8,128)(2,1)S(1)}, bf16[8,128,128]{2,1,0:T(8,128)(2,1)}, u32[]{:S(2)}) copy-start(bf16[8,128,128]{2,1,0:T(8,128)(2,1)} %get-tuple-element.83.refs_7_) | copy-start | bytes 786436
  102.8 14.5 %copy-start.2 = (bf16[8,128,128]{2,1,0:T(8,128)(2,1)S(1)}, bf16[8,128,128]{2,1,0:T(8,128)(2,1)}, u32[]{:S(2)}) copy-start(bf16[8,128,128]{2,1,0:T(8,128)(2,1)} %get-tuple-element.82.refs_6_) | copy-start | bytes 786436
  114.1 3.2 %collective-permute-start.9 = (bf16[16,128,128]{2,1,0:T(8,128)(2,1)}, bf16[16,128,128]{2,1,0:T(8,128)(2,1)S(1)}, u32[]{:S(2)}, u32[]{:S(2)}) collective-permute-start(bf16[16,128,128]{2,1,0:T(8,128)(2,1)} %get-tuple-element.69), channel_id=1, source_target_pairs={{0,1},{1,0},{2,3},{3,2},{4,5},{5,4},{6,7},{7,6},{8,9},{9,8},{10,11... | collective-permute-start | bytes 1572872 | tf_op jit(solution)/shard_map/ppermute | solution.py:590

commit v4 on v0

--- a/solution.py
+++ b/solution.py
@@ -42,7 +42,7 @@
 
         @pl.when(here >= 0)
         def _():
-            named[here % KB] = 1
+            named[here % KB] = named[here % KB] + 1
 
         return carry
 
@@ -52,7 +52,7 @@
 
 def for_wanted(column, named, rcap, action):
     def visit(slot, number):
-        wanted = (column(slot) >= 0) & (named[slot // rcap] > 0)
+        wanted = column(slot) >= 0
 
         @pl.when(wanted)
         def _():
@@ -60,7 +60,11 @@
 
         return number + wanted.astype(jnp.int32)
 
-    return lax.fori_loop(0, KB * rcap, visit, 0)
+    def visit_row(j, match, number):
+        return lax.fori_loop(j * rcap, jnp.where(match, (j + 1) * rcap, j * rcap), visit, number)
+
+    count = lax.fori_loop(0, KB, lambda j, n: visit_row(j, named[j] > 1, n), jnp.int32(0))
+    return lax.fori_loop(0, KB, lambda j, n: visit_row(j, named[j] == 1, n), count)
 
 
 def pack_main(spot, tables, strips, guests, *refs):
@@ -208,12 +212,15 @@
     lax.fori_loop(0, slots, sort, 0)
 
 
-def clear(right, low):
+def clear(right, wanted):
     def one(j, carry):
-        right[j] = jnp.zeros(right.shape[1:], right.dtype)
-        return carry
-
-    lax.fori_loop(low, KB, one, 0)
+        @pl.when(wanted(j))
+        def _():
+            right[j] = jnp.zeros(right.shape[1:], right.dtype)
+
+        return carry
+
+    lax.fori_loop(0, KB, one, 0)
 
 
 def add_rows(left, right, total, order, first):
@@ -262,11 +269,11 @@
         left_copy.start()
         table_copy = pltpu.make_async_copy(tables, table, sem_table)
         table_copy.start()
-        clear(right, 0)
         table_copy.wait()
         place = places_in(table, 0, spot[1])
         column = columns_in(table, rcap, spot[1])
         mark_rows(place, slots, named)
+        clear(right, lambda j: named[j] > 0)
 
         def fetch(slot, number):
             target = place_at(right, slot // rcap * NJ + column(slot))
@@ -308,8 +315,7 @@
     return whole
 
 
-def start_right(sources, begin, count, target, right, sem):
-    clear(right, jnp.where(count > begin, target[begin] // NJ, KB))
+def start_right(sources, count, target, right, sem):
     for blocks, low, start, stop in sources:
 
         def fetch(number, carry):
@@ -389,11 +395,11 @@
     lax.fori_loop(0, RB, start_prev, 0)
     whole = start_left(shifted, parts, left, flags[0] > 0, sem_left)
     fetched = jnp.minimum(count, end)
-    start_right([(piece, -shift, 0, end)], 0, fetched, target, right, sem_right)
+    mark_targets(target, 0, fetched, touched)
+    clear(right, lambda j: touched[j] > 0)
+    start_right([(piece, -shift, 0, end)], fetched, target, right, sem_right)
     arrive.wait()
     leave.start()
-
-    mark_targets(target, 0, fetched, touched)
     mark_targets(target, end, count, later)
     mark_open(order, first, later, open_row)
     whole.wait()
@@ -470,7 +476,8 @@
         high = low + blocks.shape[0]
         sources.append((blocks, low, low, high))
         low = high
-    start_right(sources, begin, count, target, right, sem_right)
+    clear(right, lambda j: touched[j] > 0)
+    start_right(sources, count, target, right, sem_right)
 
     def out_copy(row):
         return pltpu.make_async_copy(short.at[row], strip_of(out, row, size), sem_out.at[row])

time: 121 us -> 121 us (level); the launches traced: 121 us -> 119 us
  Pallas kernels: 50.9 us -> 49.4 us
  transfers between devices with their start and end apart: 9 -> 9, of which waited for: 3 -> 3; matrix products, arithmetic and copies ran while one was open for 8% -> 8% of each run, Pallas kernels for 36% -> 37%
where the time goes in v4:
time: 121 us; the launch traced here: 119 us
  Pallas kernels  49.4 us (41%)
  waiting for transfers between devices  39.9 us (33%)
  starting transfers between devices  17.2 us (14%)
  local copies, waits for them, and re-layouts  6.45 us (5%)
  other arithmetic  4.2 us (3%)
  between operations  2.17 us (2%)
    ppermute x2, waiting for transfers between devices, to_row_before(): lax.ppermute(blocks, 'row', [(i, (i - 1) % rows_count) for i in range(row...  31.2 us
    pallas_call x1, Pallas kernels, step_call(): pl.pallas_call(kernel, out_shape=out_shape, grid_spec=pltpu.PrefetchScala...  19.6 us
    pallas_call x2, Pallas kernels, finish_call(): pl.pallas_call(kernel, out_shape=out_shape, grid_spec=pltpu.PrefetchScala...  15 us
    pallas_call x2, Pallas kernels, pack(): pl.pallas_call(kernel, out_shape=[pltpu.HBM((n, size, size), strips.dtype...  13.1 us
    all_to_all x1, waiting for transfers between devices, local(): lax.all_to_all(jnp.concatenate([a_send[0, 0], wrapped], axis=1), both, sp...  8.73 us
    all_to_all x1, starting transfers between devices, local(): lax.all_to_all(jnp.concatenate([a_send[0, 0], wrapped], axis=1), both, sp...  6.98 us
    all_to_all x1, starting transfers between devices, local(): lax.all_to_all(table_for_all(a_where, by_slot), both, split_axis=0, conca...  5.84 us
    ppermute x2, starting transfers between devices, local(): lax.ppermute(part, 'col', [(i, last)])  3.1 us
  transfers between devices with their start and end apart: 9, of which 3 were waited for; matrix products, arithmetic and copies ran while one was open for 8% of the time, Pallas kernels for 37%

profile of v4, /device:TPU:30, one launch (start us, length us, event | category | flops | bytes accessed | tf_op | source)
XLA Modules:
  0.0 119.3 jit_solution(4087776163700816409)
XLA Ops:
  0.0 1.6 %shard_map.46 = s32[32,2,128]{2,1,0:T(2,128)} custom-call(s32[2,1,32]{2,1,0:T(1,128)} %where_ref.1, s32[8,16]{1,0:T(8,128)} %bitcast.58), custom_call_target="tpu_custom_call" | custom-call | tf_op jit(solution)/shard_map/pallas_call | solution.py:565
  1.6 5.8 %all-to-all-start = ((s32[32,2,128]{2,1,0:T(2,128)}), s32[32,2,128]{2,1,0:T(2,128)S(1)}, u32[]{:S(2)}, u32[]{:S(2)}) async-start(s32[32,2,128]{2,1,0:T(2,128)} %shard_map.46), calls=%async_computation | async-start | bytes 65536 | tf_op jit(solution)/shard_map/all_to_all | solution.py:606
  7.4 1.7 %slice_bitcast_fusion = (bf16[32,128,128]{2,1,0:T(8,128)(2,1)S(1)}, bf16[1,1,32,128,128]{4,3,2,1,0:T(8,128)(2,1)S(1)}) fusion(bf16[2,1,32,128,128]{4,3,2,1,0:T(8,128)(2,1)} %param.10), kind=kLoop, calls=%fused_computation.1 | loop fusion | bytes 4194304 | tf_op jit(solution)/shard_map/squeeze | solution.py:637
  9.2 1.2 pad_maximum_fusion
  10.4 0.0 all-to-all-done.tables
  10.4 7.0 %all-to-all-start.1 = ((bf16[32,160,128]{2,1,0:T(8,128)(2,1)}), bf16[32,160,128]{2,1,0:T(8,128)(2,1)S(1)}, u32[]{:S(2)}, u32[]{:S(2)}) async-start(bf16[32,160,128]{2,1,0:T(8,128)(2,1)} %pad_maximum_fusion), calls=%async_computation.1 | async-start | bytes 2621440 | tf_op jit(solution)/shard_map/all_to_all | solution.py:636
  17.4 0.1 copy.34
  17.5 0.1 copy.37
  17.7 0.1 slice.93
  17.7 0.1 copy.39
  17.8 0.1 copy.38
  18.0 0.6 fusion.1
  18.6 0.2 fusion.3
  18.9 0.1 copy.40
  19.0 0.7 subtract_reduce_fusion
  19.7 0.1 copy.41
  19.8 0.7 fusion.5
  20.4 1.4 %stack.32.spot = s32[7]{0:T(128)S(1)} concatenate(s32[1]{0:T(128)} %bitcast, s32[1]{0:T(128)} %bitcast.1, s32[1]{0:T(128)} %bitcast.2, s32[1]{0:T(128)} %bitcast.3, s32[1]{0:T(128)} %bitcast.4, s32[1]{0:T(128)} %bitcast.17, s32[1]{0:T(128)} %bitcast.18), dimensions={0} | concatenate | bytes 56 | tf_op jit(solution)/shard_map/stack | solution.py:624
  21.8 6.0 %shard_map.48 = (bf16[16,128,128]{2,1,0:T(8,128)(2,1)}, bf16[8,128,128]{2,1,0:T(8,128)(2,1)}, bf16[8,128,128]{2,1,0:T(8,128)(2,1)}, bf16[24,128,128]{2,1,0:T(8,128)(2,1)}) custom-call(s32[7]{0:T(128)S(1)} %stack.32.spot, s32[32,2,128]{2,1,0:T(2,128)S(1)} %all-to-all-done.tables, bf16[128,128,128]{2,1,0:T(8,128)(2,1)} %bitcast.43), custom_call_target="tpu_custom_call" | custom-call | bytes 3670016 | tf_op jit(solution)/shard_map/pallas_call | solution.py:144
  27.9 0.1 collective-permute-start.6
  29.9 0.7 slice_bitcast_fusion.5.refs_0_
  30.6 0.7 slice_bitcast_fusion.3
  31.3 0.0 collective-permute-done.6.guests
  31.3 7.1 %shard_map.49 = (bf16[64,128,128]{2,1,0:T(8,128)(2,1)}, bf16[24,128,128]{2,1,0:T(8,128)(2,1)}) custom-call(s32[7]{0:T(128)S(1)} %stack.32.spot, s32[32,2,128]{2,1,0:T(2,128)S(1)} %all-to-all-done.tables, bf16[128,128,128]{2,1,0:T(8,128)(2,1)} %bitcast.44, bf16[16,128,128]{2,1,0:T(8,128)(2,1)S(1)} %collective-permute-done.6.guests, ...), custom_call_target="tpu_custom_call" | custom-call | bytes 5767168 | tf_op jit(solution)/shard_map/pallas_call | solution.py:144
  38.4 8.7 %all-to-all-done.1.received = bf16[32,160,128]{2,1,0:T(8,128)(2,1)S(1)} async-done(((bf16[32,160,128]{2,1,0:T(8,128)(2,1)}), bf16[32,160,128]{2,1,0:T(8,128)(2,1)S(1)}, u32[]{:S(2)}, u32[]{:S(2)}) %all-to-all-start.1) | async-done | bytes 1310752 | tf_op jit(solution)/shard_map/all_to_all | solution.py:636
  47.1 0.6 slice_bitcast_fusion.2.refs_2_
  47.7 0.4 collective-permute-start.7
  48.1 0.0 collective-permute-start.3
  48.1 2.4 %collective-permute-start.5 = (bf16[32,32,128]{2,1,0:T(8,128)(2,1)S(1)}, bf16[32,32,128]{2,1,0:T(8,128)(2,1)S(1)}, u32[]{:S(2)}, u32[]{:S(2)}) collective-permute-start(bf16[32,32,128]{2,1,0:T(8,128)(2,1)S(1)} %slice.96.refs_3_), channel_id=1, source_target_pairs={{2,3},{6,7},{10,11},{14,15},{18,19},{22,23},{26,27},{30,31}} | collective-permute-start | bytes 786440 | tf_op jit(solution)/shard_map/ppermute | solution.py:662
  50.5 0.7 collective-permute-start.4
  51.2 0.7 collective-permute-start.8
  51.9 1.4 %pad_add_fusion.1.flags = s32[3]{0:T(128)S(1)} fusion(s32[1]{0:T(128)} %bitcast.25, s32[1]{0:T(128)} %bitcast.24, s32[1]{0:T(128)} %bitcast.23), kind=kLoop, calls=%fused_computation.23 | loop fusion | flops 6 | bytes 24 | tf_op jit(solution)/shard_map/stack | solution.py:689
  53.3 19.6 %shard_map.47 = (f32[2048,1024]{1,0:T(8,128)}, s32[32]{0:T(128)S(1)}, s32[19]{0:T(128)S(1)}, s32[128]{0:T(128)S(1)}) custom-call(s32[7]{0:T(128)S(1)} %stack.32.spot, s32[32,2,128]{2,1,0:T(2,128)S(1)} %all-to-all-done.tables, bf16[32,160,128]{2,1,0:T(8,128)(2,1)S(1)} %all-to-all-done.1.received, bf16[128,128,128]{2,1,0:T(8,128)(2,1)} %bitcast.45), custom_call_target="tpu_custom_call" | custom-call | flops 805306368 | bytes 16777216 | tf_op jit(solution)/shard_map/pallas_call | solution.py:510
  72.9 0.0 collective-permute-done.5.refs_2_
  72.9 0.0 collective-permute-done.4.refs_1_
  73.0 0.0 collective-permute-done.3.refs_0_
  73.0 26.2 %collective-permute-done.7.refs_4_ = bf16[64,128,128]{2,1,0:T(8,128)(2,1)} collective-permute-done((bf16[64,128,128]{2,1,0:T(8,128)(2,1)}, bf16[64,128,128]{2,1,0:T(8,128)(2,1)}, u32[]{:S(2)}, u32[]{:S(2)}) %collective-permute-start.7) | collective-permute-done | bytes 2097184 | tf_op jit(solution)/shard_map/ppermute | solution.py:642
  99.2 0.0 copy-start
  99.2 0.0 copy-start.1
  99.2 0.0 copy-start.2
  99.2 10.9 %shard_map.51 = (f32[2048,1024]{1,0:T(8,128)}, bf16[2048,1024]{1,0:T(8,128)(2,1)}, bf16[16,128,128]{2,1,0:T(8,128)(2,1)}, s32[16]{0:T(128)S(1)}, s32[16]{0:T(128)S(1)}) custom-call(s32[32]{0:T(128)S(1)} %get-tuple-element.55.order, s32[19]{0:T(128)S(1)} %get-tuple-element.56.first, s32[128]{0:T(128)S(1)} %get-tuple-element.57.target, ...), custom_call_target="tpu_custom_call" | custom-call | flops 536870912 | bytes 12582912 | tf_op jit(solution)/shard_map/pallas_call | solution.py:693
  110.1 0.1 collective-permute-start.9
  110.2 5.0 %collective-permute-done.8.refs_4_ = bf16[24,128,128]{2,1,0:T(8,128)(2,1)} collective-permute-done((bf16[24,128,128]{2,1,0:T(8,128)(2,1)}, bf16[24,128,128]{2,1,0:T(8,128)(2,1)}, u32[]{:S(2)}, u32[]{:S(2)}) %collective-permute-start.8) | collective-permute-done | bytes 786464 | tf_op jit(solution)/shard_map/ppermute | solution.py:642
  115.2 0.0 collective-permute-done.9.refs_5_
  115.2 0.0 copy-done
  115.2 0.0 copy-done.1
  115.2 0.0 copy-done.2
  115.2 4.1 %shard_map.52 = bf16[2048,1024]{1,0:T(8,128)(2,1)} custom-call(s32[32]{0:T(128)S(1)} %get-tuple-element.55.order, s32[19]{0:T(128)S(1)} %get-tuple-element.56.first, s32[128]{0:T(128)S(1)} %get-tuple-element.57.target, s32[3]{0:T(128)S(1)} %pad_add_fusion.1.flags, s32[16]{0:T(128)S(1)} %get-tuple-element.66.touched, ...), custom_call_target="tpu_custom_call", output_to_operand_aliasing={{}: (16, {})} | custom-call | flops 536870912 | bytes 12582912 | tf_op jit(solution)/shard_map/pallas_call | solution.py:693
  (17 shorter events, 0.2 us)
Async XLA Ops:
  1.6 8.8 %all-to-all-start = ((s32[32,2,128]{2,1,0:T(2,128)}), s32[32,2,128]{2,1,0:T(2,128)S(1)}, u32[]{:S(2)}, u32[]{:S(2)}) async-start(s32[32,2,128]{2,1,0:T(2,128)} %shard_map.46), calls=%async_computation | async-start | bytes 65536 | tf_op jit(solution)/shard_map/all_to_all | solution.py:606
  10.4 36.7 %all-to-all-start.1 = ((bf16[32,160,128]{2,1,0:T(8,128)(2,1)}), bf16[32,160,128]{2,1,0:T(8,128)(2,1)S(1)}, u32[]{:S(2)}, u32[]{:S(2)}) async-start(bf16[32,160,128]{2,1,0:T(8,128)(2,1)} %pad_maximum_fusion), calls=%async_computation.1 | async-start | bytes 2621440 | tf_op jit(solution)/shard_map/all_to_all | solution.py:636
  27.9 3.4 %collective-permute-start.6 = (bf16[16,128,128]{2,1,0:T(8,128)(2,1)}, bf16[16,128,128]{2,1,0:T(8,128)(2,1)S(1)}, u32[]{:S(2)}, u32[]{:S(2)}) collective-permute-start(bf16[16,128,128]{2,1,0:T(8,128)(2,1)} %get-tuple-element.58), channel_id=1, source_target_pairs={{0,1},{1,0},{2,3},{3,2},{4,5},{5,4},{6,7},{7,6},{8,9},{9,8},{10,11... | collective-permute-start | bytes 1572872 | tf_op jit(solution)/shard_map/ppermute | solution.py:591
  47.7 51.5 %collective-permute-start.7 = (bf16[64,128,128]{2,1,0:T(8,128)(2,1)}, bf16[64,128,128]{2,1,0:T(8,128)(2,1)}, u32[]{:S(2)}, u32[]{:S(2)}) collective-permute-start(bf16[64,128,128]{2,1,0:T(8,128)(2,1)} %get-tuple-element.64), channel_id=1, source_target_pairs={{0,28},{4,0},{8,4},{12,8},{16,12},{20,16},{24,20},{28,24},{1,29},{... | collective-permute-start | bytes 6291464 | tf_op jit(solution)/shard_map/ppermute | solution.py:642
  48.1 24.9 %collective-permute-start.3 = (bf16[32,160,128]{2,1,0:T(8,128)(2,1)S(1)}, bf16[32,160,128]{2,1,0:T(8,128)(2,1)S(1)}, u32[]{:S(2)}, u32[]{:S(2)}) collective-permute-start(bf16[32,160,128]{2,1,0:T(8,128)(2,1)S(1)} %all-to-all-done.1.received), channel_id=1, source_target_pairs={{0,3},{1,0},{2,1},{3,2},{4,7},{5,4},{6,5},{7,6},{8,11},{9,8},{10,9... | collective-permute-start | bytes 3932168 | tf_op jit(solution)/shard_map/ppermute | solution.py:658
  48.1 24.8 %collective-permute-start.5 = (bf16[32,32,128]{2,1,0:T(8,128)(2,1)S(1)}, bf16[32,32,128]{2,1,0:T(8,128)(2,1)S(1)}, u32[]{:S(2)}, u32[]{:S(2)}) collective-permute-start(bf16[32,32,128]{2,1,0:T(8,128)(2,1)S(1)} %slice.96.refs_3_), channel_id=1, source_target_pairs={{2,3},{6,7},{10,11},{14,15},{18,19},{22,23},{26,27},{30,31}} | collective-permute-start | bytes 786440 | tf_op jit(solution)/shard_map/ppermute | solution.py:662
  50.5 22.4 %collective-permute-start.4 = (bf16[32,32,128]{2,1,0:T(8,128)(2,1)S(1)}, bf16[32,32,128]{2,1,0:T(8,128)(2,1)S(1)}, u32[]{:S(2)}, u32[]{:S(2)}) collective-permute-start(bf16[32,32,128]{2,1,0:T(8,128)(2,1)S(1)} %slice.96.refs_3_), channel_id=1, source_target_pairs={{1,3},{5,7},{9,11},{13,15},{17,19},{21,23},{25,27},{29,31}} | collective-permute-start | bytes 786440 | tf_op jit(solution)/shard_map/ppermute | solution.py:662
  51.2 63.9 %collective-permute-start.8 = (bf16[24,128,128]{2,1,0:T(8,128)(2,1)}, bf16[24,128,128]{2,1,0:T(8,128)(2,1)}, u32[]{:S(2)}, u32[]{:S(2)}) collective-permute-start(bf16[24,128,128]{2,1,0:T(8,128)(2,1)} %get-tuple-element.68), channel_id=1, source_target_pairs={{0,28},{4,0},{8,4},{12,8},{16,12},{20,16},{24,20},{28,24},{1,29},{... | collective-permute-start | bytes 2359304 | tf_op jit(solution)/shard_map/ppermute | solution.py:642
  99.2 16.0 %copy-start = (bf16[24,128,128]{2,1,0:T(8,128)(2,1)S(1)}, bf16[24,128,128]{2,1,0:T(8,128)(2,1)}, u32[]{:S(2)}) copy-start(bf16[24,128,128]{2,1,0:T(8,128)(2,1)} %get-tuple-element.84.refs_8_) | copy-start | bytes 2359300
  99.2 16.0 %copy-start.1 = (bf16[8,128,128]{2,1,0:T(8,128)(2,1)S(1)}, bf16[8,128,128]{2,1,0:T(8,128)(2,1)}, u32[]{:S(2)}) copy-start(bf16[8,128,128]{2,1,0:T(8,128)(2,1)} %get-tuple-element.83.refs_7_) | copy-start | bytes 786436
  99.2 16.0 %copy-start.2 = (bf16[8,128,128]{2,1,0:T(8,128)(2,1)S(1)}, bf16[8,128,128]{2,1,0:T(8,128)(2,1)}, u32[]{:S(2)}) copy-start(bf16[8,128,128]{2,1,0:T(8,128)(2,1)} %get-tuple-element.82.refs_6_) | copy-start | bytes 786436
  110.1 5.1 %collective-permute-start.9 = (bf16[16,128,128]{2,1,0:T(8,128)(2,1)}, bf16[16,128,128]{2,1,0:T(8,128)(2,1)S(1)}, u32[]{:S(2)}, u32[]{:S(2)}) collective-permute-start(bf16[16,128,128]{2,1,0:T(8,128)(2,1)} %get-tuple-element.69), channel_id=1, source_target_pairs={{0,1},{1,0},{2,3},{3,2},{4,5},{5,4},{6,7},{7,6},{8,9},{9,8},{10,11... | collective-permute-start | bytes 1572872 | tf_op jit(solution)/shard_map/ppermute | solution.py:591
